TPU v7x, 32 devices: a whole 2x2x4 slice. The times are simulated.
32 devices in a mesh: fsdp: 32 (over z, y, x, core).
Axes of the slice: x: 2, y: 2, z: 4, core: 2. Of those that a mesh axis runs over, the one named last changes fastest.
Arguments:
- tokens: bfloat16 [8192, 1024], P('fsdp'), may hold values from -6 to 6
- w_query: bfloat16 [1024, 2048], P('fsdp'), may hold values from -0.1875 to 0.1875
- w_key: bfloat16 [1024, 1024], P('fsdp'), may hold values from -0.1875 to 0.1875
- w_value: bfloat16 [1024, 1024], P('fsdp'), may hold values from -0.1875 to 0.1875
- w_output: bfloat16 [2048, 1024], P(None, 'fsdp'), may hold values from -1 to 1
- w_gate: bfloat16 [1024, 3072], P('fsdp'), may hold values from -0.1875 to 0.1875
- w_up: bfloat16 [1024, 3072], P('fsdp'), may hold values from -0.1875 to 0.1875
- w_down: bfloat16 [3072, 1024], P(None, 'fsdp'), may hold values from -0.109375 to 0.109375
- norm_gains: bfloat16 [2304], P('fsdp'), may hold values from 0.099609375 to 1.8984375
- seq_lens: int32 [32, 4], P('fsdp'), may hold values from 0 to 256, as said below
- cotangent: bfloat16 [8192, 1024], P('fsdp'), may hold values from -6 to 6
Outputs:
- out: bfloat16 [8192, 1024], P('fsdp')
- grad_tokens: float32 [8192, 1024], P('fsdp')
- grad_query: float32 [1024, 2048], P('fsdp')
- grad_key: float32 [1024, 1024], P('fsdp')
- grad_value: float32 [1024, 1024], P('fsdp')
- grad_output: float32 [2048, 1024], P(None, 'fsdp')
- grad_gate: float32 [1024, 3072], P('fsdp')
- grad_up: float32 [1024, 3072], P('fsdp')
- grad_down: float32 [3072, 1024], P(None, 'fsdp')
- grad_gains: float32 [2304], P('fsdp')
Inputs may be any that keep to these rules, and one draw needn't show every extreme that they name: `seq_lens`: row r lists the lengths of the sequences of device r; each row sums to 64 to 256; a length 0 marks an unused slot; in every draw one row is a single sequence of 256 tokens.
All inputs are finite; a program needn't handle non-finite values.
Results may differ from a plain program's by a relative error of at most 0.012.
The roundings to bfloat16 on the way count: a program that leaves them out, or rounds other values in their place, can miss the bound.
Values may be sent and summed in bfloat16 or wider, within the bound.
A program may use at most 256 MiB of HBM per device.

v0:
```python
import jax
import jax.numpy as jnp
from jax import lax
from jax.sharding import PartitionSpec as P

QUERY_HEADS = 16
VALUE_HEADS = 8
HEAD_WIDTH = 128
SLOTS = 4


EPSILON = 1e-06
ROPE_BASE = 1000000.0
MASKED_SCORE = -1e30


def arrange(lengths, token_budget):
    seq_ends = jnp.cumsum(lengths)
    seq_starts = seq_ends - lengths
    places = jnp.arange(token_budget, dtype=jnp.int32)
    segment = jnp.sum((places[:, None] >= seq_ends[None, :]).astype(jnp.int32), axis=1)
    owned_by = segment[:, None] == jnp.arange(SLOTS, dtype=jnp.int32)[None, :]
    first_place = jnp.sum(jnp.where(owned_by, seq_starts[None, :], 0), axis=1)
    return (segment, places - first_place)


def rope_tables(position):
    half_width = HEAD_WIDTH // 2
    inverse = ROPE_BASE ** (-(jnp.arange(half_width, dtype=jnp.float32) * 2.0 / HEAD_WIDTH))
    angles = position.astype(jnp.float32)[:, None] * inverse[None, :]
    angles = jnp.concatenate([angles, angles], axis=-1)
    return (jnp.cos(angles)[:, None, :], jnp.sin(angles)[:, None, :])


def apply_rotary(values, cosine_lookup, sine_lookup):
    half_width = values.shape[-1] // 2
    turned = jnp.concatenate([-values[..., half_width:], values[..., :half_width]], axis=-1)
    return values * cosine_lookup + turned * sine_lookup


def rotate_back(grads, cosine_lookup, sine_lookup):
    half_width = grads.shape[-1] // 2
    turned = grads * sine_lookup
    return grads * cosine_lookup + jnp.concatenate(
        [turned[..., half_width:], -turned[..., :half_width]], axis=-1
    )


def normalize(values):
    row_scale = lax.rsqrt(jnp.mean(values * values, axis=-1, keepdims=True) + EPSILON)
    return (values * row_scale, row_scale)


def norm_back(grads, unit_vals, row_scale):
    return row_scale * (grads - unit_vals * jnp.mean(grads * unit_vals, axis=-1, keepdims=True))


def apply_projection(left, weight):
    return jnp.dot(left, weight, preferred_element_type=jnp.float32)


def back_project(grads, weight):
    return jnp.einsum("tj,ij->ti", grads, weight, preferred_element_type=jnp.float32)


def contract(left, right):
    return jnp.einsum("ti,tj->ij", left, right, preferred_element_type=jnp.float32)


def split_gains(gain_all, model_width):
    gain_all = gain_all.astype(jnp.float32)
    return (
        gain_all[:model_width],
        gain_all[model_width : 2 * model_width],
        gain_all[2 * model_width : 2 * model_width + HEAD_WIDTH],
        gain_all[2 * model_width + HEAD_WIDTH :],
    )


def block_scores(query_block, key_block, seg_rows, seg_keys, first_row):
    row_count = query_block.shape[0]
    key_count = key_block.shape[0]
    raw = jnp.einsum("qkgd,lkd->kgql", query_block, key_block, preferred_element_type=jnp.float32)
    row_at = first_row + jnp.arange(row_count, dtype=jnp.int32)
    key_at = jnp.arange(key_count, dtype=jnp.int32)
    allowed = (seg_rows[:, None] == seg_keys[None, :]) & (row_at[:, None] >= key_at[None, :])
    return jnp.where(allowed[None, None], raw * HEAD_WIDTH ** (-0.5), MASKED_SCORE)


def local(
    tokens, w_query, w_key, w_value, w_output, w_gate, w_up, w_down, norm_gains, seq_lens, cotangent
):
    attn_parts = (w_query, w_key, w_value, w_output, norm_gains)
    ffn_parts = (w_gate, w_up, w_down)
    query_w, key_matrix, value_matrix, out_w, gain_all = (
        lax.all_gather(attn_parts[0], "fsdp", axis=0, tiled=True),
        lax.all_gather(attn_parts[1], "fsdp", axis=0, tiled=True),
        lax.all_gather(attn_parts[2], "fsdp", axis=0, tiled=True),
        lax.all_gather(attn_parts[3], "fsdp", axis=1, tiled=True),
        lax.all_gather(attn_parts[4], "fsdp", axis=0, tiled=True),
    )
    gate_w, up_w, down_w = (
        lax.all_gather(ffn_parts[0], "fsdp", axis=0, tiled=True),
        lax.all_gather(ffn_parts[1], "fsdp", axis=0, tiled=True),
        lax.all_gather(ffn_parts[2], "fsdp", axis=1, tiled=True),
    )
    token_budget = tokens.shape[0]
    model_width = tokens.shape[1]
    hidden_width = gate_w.shape[1]
    query_group_width = QUERY_HEADS // VALUE_HEADS
    rows_per_block = min(512, token_budget)
    attn_gain, ffn_gain, query_norm_weight, key_gain = split_gains(gain_all, model_width)
    segment, position = arrange(seq_lens[0], token_budget)
    live_rows = (segment < SLOTS).astype(jnp.float32)[:, None]
    cosine_lookup, sine_lookup = rope_tables(position)
    stream = tokens.astype(jnp.float32)
    unit_in, scale_in = normalize(stream)
    rescaled_input = (unit_in * attn_gain).astype(jnp.bfloat16)
    query_unrotated = apply_projection(rescaled_input, query_w).reshape(
        token_budget, QUERY_HEADS, HEAD_WIDTH
    )
    key_unrotated = apply_projection(rescaled_input, key_matrix).reshape(
        token_budget, VALUE_HEADS, HEAD_WIDTH
    )
    value_reduced = (
        apply_projection(rescaled_input, value_matrix)
        .astype(jnp.bfloat16)
        .reshape(token_budget, VALUE_HEADS, HEAD_WIDTH)
    )
    query_unit, query_scale = normalize(query_unrotated)
    key_unit, key_scale = normalize(key_unrotated)
    query_rotated = apply_rotary(query_unit * query_norm_weight, cosine_lookup, sine_lookup).astype(
        jnp.bfloat16
    )
    query_rotated = query_rotated.reshape(token_budget, VALUE_HEADS, query_group_width, HEAD_WIDTH)
    key_rot = apply_rotary(key_unit * key_gain, cosine_lookup, sine_lookup).astype(jnp.bfloat16)
    block_no = 0
    first_row = block_no * rows_per_block
    scores = block_scores(query_rotated, key_rot, segment, segment, first_row)
    row_top = jnp.max(scores, axis=-1, keepdims=True)
    lifted = jnp.exp(scores - row_top)
    row_mass = jnp.sum(lifted, axis=-1, keepdims=True)
    prob_low = (lifted / row_mass).astype(jnp.bfloat16)
    mixed = jnp.einsum(
        "kgql,lkd->qkgd", prob_low, value_reduced, preferred_element_type=jnp.float32
    )
    pieces = mixed.reshape(rows_per_block, QUERY_HEADS * HEAD_WIDTH)
    log_mass = [row_top + jnp.log(row_mass)]
    attended = pieces.astype(jnp.bfloat16)
    branch = apply_projection(attended, out_w)
    middle = stream + live_rows * branch
    unit_mid, scale_mid = normalize(middle)
    normed_mid = (unit_mid * ffn_gain).astype(jnp.bfloat16)
    gate_pre = apply_projection(normed_mid, gate_w)
    up_pre = apply_projection(normed_mid, up_w)
    gate_sig = jax.nn.sigmoid(gate_pre)
    gate_act = gate_pre * gate_sig
    hidden = (gate_act * up_pre).astype(jnp.bfloat16)
    result = middle + live_rows * apply_projection(hidden, down_w)
    gate_w, up_w, down_w = (
        lax.all_gather(ffn_parts[0], "fsdp", axis=0, tiled=True),
        lax.all_gather(ffn_parts[1], "fsdp", axis=0, tiled=True),
        lax.all_gather(ffn_parts[2], "fsdp", axis=1, tiled=True),
    )
    grad_out = cotangent.astype(jnp.float32)
    grad_ffn = (live_rows * grad_out).astype(jnp.bfloat16)
    grad_hidden = back_project(grad_ffn, down_w)
    grad_up_pre = (grad_hidden * gate_act).astype(jnp.bfloat16)
    grad_gate_pre = (grad_hidden * up_pre * gate_sig * (1.0 + gate_pre * (1.0 - gate_sig))).astype(
        jnp.bfloat16
    )
    owned_all = lax.psum_scatter(
        jnp.concatenate(
            [
                contract(normed_mid, grad_gate_pre),
                contract(normed_mid, grad_up_pre),
                contract(grad_ffn, hidden),
            ],
            axis=1,
        ),
        "fsdp",
        scatter_dimension=0,
        tiled=True,
    )
    owned_gate = owned_all[:, :hidden_width]
    owned_up = owned_all[:, hidden_width : 2 * hidden_width]
    owned_down = owned_all[:, 2 * hidden_width :].T
    grad_mid_norm = back_project(grad_gate_pre, gate_w) + back_project(grad_up_pre, up_w)
    grad_ffn_gain = jnp.sum(grad_mid_norm * unit_mid, axis=0)
    grad_middle = grad_out + norm_back(grad_mid_norm * ffn_gain, unit_mid, scale_mid)
    query_w, key_matrix, value_matrix, out_w, gain_all = (
        lax.all_gather(attn_parts[0], "fsdp", axis=0, tiled=True),
        lax.all_gather(attn_parts[1], "fsdp", axis=0, tiled=True),
        lax.all_gather(attn_parts[2], "fsdp", axis=0, tiled=True),
        lax.all_gather(attn_parts[3], "fsdp", axis=1, tiled=True),
        lax.all_gather(attn_parts[4], "fsdp", axis=0, tiled=True),
    )
    attn_gain, ffn_gain, query_norm_weight, key_gain = split_gains(gain_all, model_width)
    grad_branch = (live_rows * grad_middle).astype(jnp.bfloat16)
    gradient_mixed_values = back_project(grad_branch, out_w).astype(jnp.bfloat16)
    block_no = 0
    first_row = block_no * rows_per_block
    scores = block_scores(query_rotated, key_rot, segment, segment, first_row)
    prob_rows = jnp.exp(scores - log_mass[block_no])
    prob_low = prob_rows.astype(jnp.bfloat16)
    row_gradient = gradient_mixed_values.reshape(
        rows_per_block, VALUE_HEADS, query_group_width, HEAD_WIDTH
    )
    grad_probs = jnp.einsum(
        "qkgd,lkd->kgql", row_gradient, value_reduced, preferred_element_type=jnp.float32
    )
    centre = jnp.sum(prob_rows * grad_probs, axis=-1, keepdims=True)
    grad_raw = (prob_rows * (grad_probs - centre) * HEAD_WIDTH ** (-0.5)).astype(jnp.bfloat16)
    query_grads = jnp.einsum(
        "kgql,lkd->qkgd", grad_raw, key_rot, preferred_element_type=jnp.float32
    )
    grad_keys = jnp.einsum(
        "kgql,qkgd->lkd", grad_raw, query_rotated, preferred_element_type=jnp.float32
    )
    value_gradient = jnp.einsum(
        "kgql,qkgd->lkd", prob_low, row_gradient, preferred_element_type=jnp.float32
    )
    grad_qrot = query_grads.reshape(token_budget, QUERY_HEADS, HEAD_WIDTH)
    grad_qhead = rotate_back(grad_qrot, cosine_lookup, sine_lookup)
    grad_query_gain = jnp.sum(grad_qhead * query_unit, axis=(0, 1))
    grad_qraw = (
        norm_back(grad_qhead * query_norm_weight, query_unit, query_scale)
        .reshape(token_budget, QUERY_HEADS * HEAD_WIDTH)
        .astype(jnp.bfloat16)
    )
    grad_khead = rotate_back(grad_keys, cosine_lookup, sine_lookup)
    grad_key_gain = jnp.sum(grad_khead * key_unit, axis=(0, 1))
    grad_kraw = (
        norm_back(grad_khead * key_gain, key_unit, key_scale)
        .reshape(token_budget, VALUE_HEADS * HEAD_WIDTH)
        .astype(jnp.bfloat16)
    )
    value_raw_gradient = value_gradient.reshape(token_budget, VALUE_HEADS * HEAD_WIDTH).astype(
        jnp.bfloat16
    )
    grad_in_norm = (
        back_project(grad_qraw, query_w)
        + back_project(grad_kraw, key_matrix)
        + back_project(value_raw_gradient, value_matrix)
    )
    grad_attn_gain = jnp.sum(grad_in_norm * unit_in, axis=0)
    grad_input = grad_middle + norm_back(grad_in_norm * attn_gain, unit_in, scale_in)
    grad_gain_all = jnp.concatenate(
        [grad_attn_gain, grad_ffn_gain, grad_query_gain, grad_key_gain], axis=0
    )
    query_width = grad_qraw.shape[1]
    key_width = grad_kraw.shape[1]
    attn_owned = lax.psum_scatter(
        jnp.concatenate(
            [
                contract(rescaled_input, grad_qraw),
                contract(rescaled_input, grad_kraw),
                contract(rescaled_input, value_raw_gradient),
                contract(grad_branch, attended),
            ],
            axis=1,
        ),
        "fsdp",
        scatter_dimension=0,
        tiled=True,
    )
    owned_query = attn_owned[:, :query_width]
    owned_key = attn_owned[:, query_width : query_width + key_width]
    owned_value = attn_owned[:, query_width + key_width : query_width + 2 * key_width]
    owned_output = attn_owned[:, query_width + 2 * key_width :].T
    owned_gains = lax.psum_scatter(grad_gain_all, "fsdp", scatter_dimension=0, tiled=True)
    return (
        result.astype(jnp.bfloat16),
        grad_input,
        owned_query,
        owned_key,
        owned_value,
        owned_output,
        owned_gate,
        owned_up,
        owned_down,
        owned_gains,
    )


def solution(mesh):
    in_specs = (
        P("fsdp", None),
        P("fsdp", None),
        P("fsdp", None),
        P("fsdp", None),
        P(None, "fsdp"),
        P("fsdp", None),
        P("fsdp", None),
        P(None, "fsdp"),
        P("fsdp"),
        P("fsdp", None),
        P("fsdp", None),
    )
    out_specs = (
        P("fsdp", None),
        P("fsdp", None),
        P("fsdp", None),
        P("fsdp", None),
        P("fsdp", None),
        P(None, "fsdp"),
        P("fsdp", None),
        P("fsdp", None),
        P(None, "fsdp"),
        P("fsdp"),
    )
    return jax.shard_map(local, mesh=mesh, in_specs=in_specs, out_specs=out_specs, check_vma=False)
```

profile of v0, /device:TPU:0, one launch (start us, length us, event | category | flops | bytes accessed | tf_op | source)
XLA Modules:
  0.0 1183.1 jit_solution(5579744552906658672)
XLA Ops:
  16.0 42.1 %all-reduce = bf16[2304]{0:T(1024)(128)(2,1)S(1)} all-reduce(bf16[2304]{0:T(1024)(128)(2,1)S(1)} %dynamic-update-slice), channel_id=1, replica_groups=mesh['fsdp'=32] {'fsdp'}, use_global_device_ids=true, to_apply=%add | all-reduce | flops 2304 | bytes 9216
  62.9 7.2 all-gather.8.cloned.1.call-done
  70.1 2.5 fusion.34
  73.5 54.9 %all-gather.10.cloned.1.call-done = bf16[1024,1024]{1,0:T(8,128)(2,1)} async-done(((bf16[32,1024]{1,0:T(8,128)(2,1)}), bf16[1024,1024]{1,0:T(8,128)(2,1)}) %all-gather.10.cloned.1.call-update) | async-done | bytes 2097168 | tf_op jit(solution)/shard_map/all_gather | solution.py:97
  128.4 2.3 convolution_bitcast_fusion
  133.8 58.4 %all-gather.12.cloned.1.call-done = bf16[1024,2048]{1,0:T(8,128)(2,1)} async-done(((bf16[32,2048]{1,0:T(8,128)(2,1)}), bf16[1024,2048]{1,0:T(8,128)(2,1)}) %all-gather.12.cloned.1.call-update) | async-done | bytes 4194320 | tf_op jit(solution)/shard_map/all_gather | solution.py:96
  192.2 4.9 fusion.68
  197.1 1.9 copy.188
  201.1 2.2 mul.391
  203.3 3.3 copy.165
  213.9 41.7 %all-gather.14.cloned.1.call-done = bf16[2048,1024]{0,1:T(8,128)(2,1)} async-done(((bf16[2048,32]{0,1:T(8,128)(2,1)}), bf16[2048,1024]{0,1:T(8,128)(2,1)}) %all-gather.14.cloned.1.call-update) | async-done | bytes 4194320 | tf_op jit(solution)/shard_map/all_gather | solution.py:99
  255.6 4.1 multiply_reduce_fusion.7
  261.6 64.7 %all-gather.18.cloned.1.call-done = bf16[1024,3072]{1,0:T(8,128)(2,1)} async-done(((bf16[32,3072]{1,0:T(8,128)(2,1)}), bf16[1024,3072]{1,0:T(8,128)(2,1)}) %all-gather.18.cloned.1.call-update) | async-done | bytes 6291472 | tf_op jit(solution)/shard_map/all_gather | solution.py:104
  326.4 6.5 fusion.79
  332.9 64.2 %all-gather.16.cloned.1.call-done = bf16[1024,3072]{1,0:T(8,128)(2,1)} async-done(((bf16[32,3072]{1,0:T(8,128)(2,1)}), bf16[1024,3072]{1,0:T(8,128)(2,1)}) %all-gather.16.cloned.1.call-update) | async-done | bytes 6291472 | tf_op jit(solution)/shard_map/all_gather | solution.py:103
  397.1 6.4 fusion.78
  403.5 64.5 %all-gather.20.cloned.1.call-done = bf16[3072,1024]{0,1:T(8,128)(2,1)} async-done(((bf16[3072,32]{0,1:T(8,128)(2,1)}), bf16[3072,1024]{0,1:T(8,128)(2,1)}) %all-gather.20.cloned.1.call-update) | async-done | bytes 6291472 | tf_op jit(solution)/shard_map/all_gather | solution.py:105
  468.0 8.9 multiply_convert_fusion
  477.0 2.0 fusion.80
  479.1 5.6 multiply_reduce_fusion.4
  486.0 2.3 convolution_convert_fusion
  488.3 2.3 copy.192
  490.6 4.2 fusion.47
  496.5 9.5 broadcast_multiply_fusion.1
  505.9 9.2 fusion.18
  515.2 3.1 copy.160
  520.1 2.7 fusion.72
  522.8 3.5 copy.162
  526.3 4.1 pad_maximum_fusion.2
  530.4 3.5 copy.163
  533.9 6.4 fusion.61
  541.7 3.1 copy.191
  544.8 3.0 multiply_reduce_fusion
  548.0 2.1 fusion.62
  550.4 2.9 fusion.64
  553.5 2.0 mul.437
  556.5 4.3 fusion.11
  562.3 10.4 pad_maximum_fusion.1
  573.7 8.8 fusion.83
  582.5 7.6 fusion.82
  590.1 7.6 fusion.50
  597.7 28.8 %pad_maximum_fusion = f32[1024,9216]{1,0:T(8,128)} fusion(f32[1024,3072]{1,0:T(8,128)} %fusion.50, f32[1024,3072]{1,0:T(8,128)} %fusion.83, f32[1024,3072]{1,0:T(8,128)} %fusion.82), kind=kLoop, calls=%fused_computation.1 | loop fusion | flops 18874368 | bytes 75497472 | tf_op jit(solution)/shard_map/concatenate | solution.py:173
  627.8 3.6 fusion.81
  634.2 43.7 %all-reduce.1 = f32[2304]{0:T(1024)S(1)} all-reduce(f32[2304]{0:T(1024)S(1)} %pad_maximum_fusion.4), channel_id=4, replica_groups=mesh['fsdp'=32] {'fsdp'}, use_global_device_ids=true, to_apply=%region_20.21.clone | all-reduce | flops 2304 | bytes 18432
  679.7 5.4 fusion.30
  685.2 132.6 %reduce-scatter.3.cloned.1.call-done = f32[32,6144]{1,0:T(8,128)} async-done(((f32[1024,6144]{1,0:T(8,128)}), f32[32,6144]{1,0:T(8,128)}) %reduce-scatter.3.cloned.1.call-update) | async-done | bytes 786448 | tf_op jit(solution)/shard_map/reduce_scatter | solution.py:253
  821.3 352.5 %reduce-scatter.5.cloned.1.call-done = f32[32,9216]{1,0:T(8,128)} async-done(((f32[1024,9216]{1,0:T(8,128)}), f32[32,9216]{1,0:T(8,128)}) %reduce-scatter.5.cloned.1.call-update) | async-done | bytes 1179664 | tf_op jit(solution)/shard_map/reduce_scatter | solution.py:172
  1173.8 2.3 slice_bitcast_fusion
  (202 shorter events, 47.9 us)
Async XLA Ops:
  7.2 62.9 %all-gather.8.cloned.1.call-start = ((), (), s32[]{:S(2)}) async-start(), calls=%async_computation.2 | async-start | bytes 2162688 | tf_op jit(solution)/shard_map/all_gather | solution.py:98
  7.9 120.5 %all-gather.10.cloned.1.call-start = ((), (), s32[]{:S(2)}) async-start(), calls=%async_computation.3 | async-start | bytes 2162688 | tf_op jit(solution)/shard_map/all_gather | solution.py:97
  8.7 183.5 %all-gather.12.cloned.1.call-start = ((), (), s32[]{:S(2)}) async-start(), calls=%async_computation.4 | async-start | bytes 4325376 | tf_op jit(solution)/shard_map/all_gather | solution.py:96
  9.4 246.2 %all-gather.14.cloned.1.call-start = ((), (), s32[]{:S(2)}) async-start(), calls=%async_computation.5 | async-start | bytes 4325376 | tf_op jit(solution)/shard_map/all_gather | solution.py:99
  10.0 316.4 %all-gather.18.cloned.1.call-start = ((), (), s32[]{:S(2)}) async-start(), calls=%async_computation.7 | async-start | bytes 6488064 | tf_op jit(solution)/shard_map/all_gather | solution.py:104
  10.6 386.6 %all-gather.16.cloned.1.call-start = ((), (), s32[]{:S(2)}) async-start(), calls=%async_computation.6 | async-start | bytes 6488064 | tf_op jit(solution)/shard_map/all_gather | solution.py:103
  11.1 456.9 %all-gather.20.cloned.1.call-start = ((), (), s32[]{:S(2)}) async-start(), calls=%async_computation.8 | async-start | bytes 6488064 | tf_op jit(solution)/shard_map/all_gather | solution.py:105
  11.9 116.5 %copy-start.2 = (bf16[256,1024]{1,0:T(8,128)(2,1)S(1)}, bf16[256,1024]{1,0:T(8,128)(2,1)}, u32[]{:S(2)}) copy-start(bf16[256,1024]{1,0:T(8,128)(2,1)} %param.11) | copy-start | bytes 1572868
  11.9 805.9 %reduce-scatter.3.cloned.1.call-start = ((), (), s32[]{:S(2)}) async-start(), calls=%async_computation.9 | async-start | bytes 25952256 | tf_op jit(solution)/shard_map/reduce_scatter | solution.py:253
  210.0 2.0 copy-start.37
  255.5 4.1 copy-start.38
  255.5 4.1 copy-start.43
  255.5 5.1 copy-start.46
  468.0 8.9 copy-start.57
  476.9 2.1 copy-start.30
  476.9 2.1 copy-start.32
  477.0 2.1 copy-start.18
  477.0 2.1 copy-start.47
  477.0 2.1 copy-start.55
  479.1 5.6 copy-start.23
  479.1 6.9 copy-start.58
  490.6 4.2 copy-start.1
  490.6 4.2 copy-start.6
  490.6 4.2 copy-start.41
  515.2 3.1 copy-start.35
  530.4 3.5 copy-start.45
  533.9 6.4 copy-start.34
  533.9 6.5 copy-start.33
  533.9 6.5 copy-start.53
  541.7 3.1 copy-start.40
  541.7 3.1 copy-start.51
  547.8 2.3 copy-start.16
  548.0 2.4 copy-start.3
  550.4 3.1 copy-start.13
  550.4 5.1 copy-start.10
  550.4 5.1 copy-start.11
  553.3 2.1 copy-start.8
  553.3 3.1 copy-start.9
  553.3 3.1 copy-start.48
  553.5 8.7 slice-start
  556.5 5.8 slice-start.1
  572.7 9.8 copy-start.31
  572.7 601.2 %reduce-scatter.5.cloned.1.call-start = ((), (), s32[]{:S(2)}) async-start(), calls=%async_computation.10 | async-start | bytes 38928384 | tf_op jit(solution)/shard_map/reduce_scatter | solution.py:172
  582.5 7.6 copy-start.24
  582.5 7.6 copy-start.28
  627.8 3.6 copy-start.7
  627.8 3.6 copy-start.14
  633.2 45.3 %copy-start.5 = (f32[256,1024]{1,0:T(8,128)S(1)}, f32[256,1024]{1,0:T(8,128)}, u32[]{:S(2)}) copy-start(f32[256,1024]{1,0:T(8,128)} %copy-done.4) | copy-start | bytes 3145732
  (22 other events, 27.2 us)
Sparse Core Ops, SparseCore 0:
  10.9 59.1 all-gather.7
  73.0 55.4 all-gather.9
  131.3 60.8 all-gather.11
  194.9 60.5 all-gather.13
  258.3 68.0 all-gather.17
  329.1 68.0 all-gather.15
  400.0 67.9 all-gather.19
  572.8 244.9 reduce-scatter.2
  825.4 348.4 reduce-scatter.4
where the time goes:
time: 1190 us; the launch traced here: 1180 us
  waiting for transfers between devices  845 us (71%)
  matrix products  121 us (10%)
  blocking collectives  85.8 us (7%)
  other arithmetic  70.5 us (6%)
  local copies, waits for them, and re-layouts  45.4 us (4%)
  between operations  15 us (1%)
    reduce_scatter x1, waiting for transfers between devices, local(): lax.psum_scatter(jnp.concatenate([contract(normed_mid, grad_gate_pre), co...  352 us
    reduce_scatter x1, waiting for transfers between devices, local(): lax.psum_scatter(jnp.concatenate([contract(rescaled_input, grad_qraw), co...  133 us
    unnamed x2, blocking collectives  85.8 us
    all_gather x1, waiting for transfers between devices, local(): lax.all_gather(ffn_parts[1], 'fsdp', axis=0, tiled=True)  64.7 us
    all_gather x1, waiting for transfers between devices, local(): lax.all_gather(ffn_parts[2], 'fsdp', axis=1, tiled=True)  64.5 us
    all_gather x1, waiting for transfers between devices, local(): lax.all_gather(ffn_parts[0], 'fsdp', axis=0, tiled=True)  64.2 us
    all_gather x1, waiting for transfers between devices, local(): lax.all_gather(attn_parts[0], 'fsdp', axis=0, tiled=True)  58.4 us
    all_gather x1, waiting for transfers between devices, local(): lax.all_gather(attn_parts[1], 'fsdp', axis=0, tiled=True)  54.9 us
  transfers between devices with their start and end apart: 9, of which 9 were waited for; matrix products, arithmetic and copies ran while one was open for 11% of the time, Pallas kernels for 0%

commit v1 on v0

v1 whole, which is shorter than its diff:
```python
import functools

import jax
import jax.numpy as jnp
from jax import lax
from jax.sharding import PartitionSpec as P

QUERY_HEADS = 16
VALUE_HEADS = 8
HEAD_WIDTH = 128
SLOTS = 4


EPSILON = 1e-06
ROPE_BASE = 1000000.0
MASKED_SCORE = -1e30


def arrange(lengths, token_budget):
    seq_ends = jnp.cumsum(lengths)
    seq_starts = seq_ends - lengths
    places = jnp.arange(token_budget, dtype=jnp.int32)
    segment = jnp.sum((places[:, None] >= seq_ends[None, :]).astype(jnp.int32), axis=1)
    owned_by = segment[:, None] == jnp.arange(SLOTS, dtype=jnp.int32)[None, :]
    first_place = jnp.sum(jnp.where(owned_by, seq_starts[None, :], 0), axis=1)
    return (segment, places - first_place)


def rope_tables(position):
    half_width = HEAD_WIDTH // 2
    inverse = ROPE_BASE ** (-(jnp.arange(half_width, dtype=jnp.float32) * 2.0 / HEAD_WIDTH))
    angles = position.astype(jnp.float32)[:, None] * inverse[None, :]
    angles = jnp.concatenate([angles, angles], axis=-1)
    return (jnp.cos(angles)[:, None, :], jnp.sin(angles)[:, None, :])


def apply_rotary(values, cosine_lookup, sine_lookup):
    half_width = values.shape[-1] // 2
    turned = jnp.concatenate([-values[..., half_width:], values[..., :half_width]], axis=-1)
    return values * cosine_lookup + turned * sine_lookup


def rotate_back(grads, cosine_lookup, sine_lookup):
    half_width = grads.shape[-1] // 2
    turned = grads * sine_lookup
    return grads * cosine_lookup + jnp.concatenate(
        [turned[..., half_width:], -turned[..., :half_width]], axis=-1
    )


def normalize(values):
    row_scale = lax.rsqrt(jnp.mean(values * values, axis=-1, keepdims=True) + EPSILON)
    return (values * row_scale, row_scale)


def norm_back(grads, unit_vals, row_scale):
    return row_scale * (grads - unit_vals * jnp.mean(grads * unit_vals, axis=-1, keepdims=True))


def apply_projection(left, weight):
    return jnp.dot(left, weight, preferred_element_type=jnp.float32)


def back_project(grads, weight):
    return jnp.einsum("tj,ij->ti", grads, weight, preferred_element_type=jnp.float32)


def contract(left, right):
    return jnp.einsum("ti,tj->ij", left, right, preferred_element_type=jnp.float32)


def split_gains(gain_all, model_width):
    gain_all = gain_all.astype(jnp.float32)
    return (
        gain_all[:model_width],
        gain_all[model_width : 2 * model_width],
        gain_all[2 * model_width : 2 * model_width + HEAD_WIDTH],
        gain_all[2 * model_width + HEAD_WIDTH :],
    )


def block_scores(query_block, key_block, seg_rows, seg_keys, first_row):
    row_count = query_block.shape[0]
    key_count = key_block.shape[0]
    raw = jnp.einsum("qkgd,lkd->kgql", query_block, key_block, preferred_element_type=jnp.float32)
    row_at = first_row + jnp.arange(row_count, dtype=jnp.int32)
    key_at = jnp.arange(key_count, dtype=jnp.int32)
    allowed = (seg_rows[:, None] == seg_keys[None, :]) & (row_at[:, None] >= key_at[None, :])
    return jnp.where(allowed[None, None], raw * HEAD_WIDTH ** (-0.5), MASKED_SCORE)


def part_orders(device_count):
    bits = device_count.bit_length() - 1
    if bits == 5:
        return [[1, 2, 3, 4], [2, 1, 3, 4], [3, 1, 2, 4]]
    chip = list(range(1, bits))
    third = (bits - 1) // 3
    return [chip, chip[third:] + chip[:third], chip[2 * third :] + chip[: 2 * third]]


def partners(device_count, bit):
    return [(i, i ^ (1 << bit)) for i in range(device_count)]


def pick_core(me, device_count, rows, core):
    model = device_count * rows
    source = jnp.arange(model, dtype=jnp.int32)[:, None]
    target = jnp.arange(model // 2, dtype=jnp.int32)[None, :]
    wanted = ((target // rows) * 2 + core) * rows + target % rows
    return (source == wanted).astype(jnp.bfloat16)


def pick_order(me, device_count, rows, order):
    half = device_count * rows // 2
    source = jnp.arange(half, dtype=jnp.int32)[:, None]
    target = jnp.arange(half, dtype=jnp.int32)[None, :]
    far = target // rows
    chip = jnp.zeros_like(far)
    last = len(order) - 1
    for place, bit in enumerate(order):
        chip = chip + (((far >> (last - place)) & 1) << (bit - 1))
    wanted = (chip ^ (me // 2)) * rows + target % rows
    return (source == wanted).astype(jnp.bfloat16)


def exact(left, onehot):
    return jnp.dot(left, onehot, preferred_element_type=jnp.float32).astype(jnp.bfloat16)


def swap(values, device_count, bit):
    return lax.ppermute(values, "fsdp", partners(device_count, bit))


def sum_to_owner(left, right, device_count, order):
    half = left.shape[1] // 2
    sent = contract(left[:, half:], right).astype(jnp.bfloat16)
    arrived = swap(sent, device_count, order[0])
    total = contract(left[:, :half], right) + arrived.astype(jnp.float32)
    for bit in order[1:]:
        half //= 2
        arrived = swap(total[half:].astype(jnp.bfloat16), device_count, bit)
        total = total[:half] + arrived.astype(jnp.float32)
    return total


def local(
    device_count,
    tokens, w_query, w_key, w_value, w_output, w_gate, w_up, w_down, norm_gains, seq_lens, cotangent
):
    me = lax.axis_index("fsdp")
    core = me % 2
    orders = part_orders(device_count)
    token_budget = tokens.shape[0]
    model_width = tokens.shape[1]
    rows = w_query.shape[0]
    qw = w_query.shape[1]
    kw = w_key.shape[1]
    ff = w_gate.shape[1]
    own_gains = norm_gains.shape[0]
    gain_block = jnp.pad(norm_gains[None, :], ((0, rows - 1), (0, 128 - own_gains)))
    gathered = lax.all_gather(
        jnp.concatenate(
            [w_query, w_key, w_value, w_output.T, w_gate, w_up, w_down.T, gain_block], axis=1
        ),
        "fsdp",
        axis=0,
        tiled=True,
    )
    at = qw + 2 * kw
    qkv_w = gathered[:, :at]
    out_wt = gathered[:, at : at + qw]
    at = at + qw
    gate_up_w = gathered[:, at : at + 2 * ff]
    at = at + 2 * ff
    down_wt = gathered[:, at : at + ff]
    at = at + ff
    gain_all = gathered[:, at:].reshape(device_count, rows, 128)[:, 0, :own_gains].reshape(-1)

    query_group_width = QUERY_HEADS // VALUE_HEADS
    rows_per_block = token_budget
    attn_gain, ffn_gain, query_norm_weight, key_gain = split_gains(gain_all, model_width)
    segment, position = arrange(seq_lens[0], token_budget)
    live_rows = (segment < SLOTS).astype(jnp.float32)[:, None]
    cosine_lookup, sine_lookup = rope_tables(position)
    pick_mine = pick_core(me, device_count, rows, core)
    pick_mate = pick_core(me, device_count, rows, 1 - core)
    picks = [pick_order(me, device_count, rows, order) for order in orders]

    def both(values):
        return jnp.concatenate([values, swap(values, device_count, 0)], axis=0)

    def both_halves(values):
        mine = exact(values, pick_mine)
        other = swap(exact(values, pick_mate), device_count, 0)
        return jnp.concatenate([mine, other], axis=0)

    stream = tokens.astype(jnp.float32)
    unit_in, scale_in = normalize(stream)
    rescaled_input = (unit_in * attn_gain).astype(jnp.bfloat16)
    qkv = apply_projection(rescaled_input, qkv_w)
    query_unrotated = qkv[:, :qw].reshape(token_budget, QUERY_HEADS, HEAD_WIDTH)
    key_unrotated = qkv[:, qw : qw + kw].reshape(token_budget, VALUE_HEADS, HEAD_WIDTH)
    value_reduced = (
        qkv[:, qw + kw :].astype(jnp.bfloat16).reshape(token_budget, VALUE_HEADS, HEAD_WIDTH)
    )
    query_unit, query_scale = normalize(query_unrotated)
    key_unit, key_scale = normalize(key_unrotated)
    query_rotated = apply_rotary(query_unit * query_norm_weight, cosine_lookup, sine_lookup).astype(
        jnp.bfloat16
    )
    query_rotated = query_rotated.reshape(token_budget, VALUE_HEADS, query_group_width, HEAD_WIDTH)
    key_rot = apply_rotary(key_unit * key_gain, cosine_lookup, sine_lookup).astype(jnp.bfloat16)
    scores = block_scores(query_rotated, key_rot, segment, segment, 0)
    row_top = jnp.max(scores, axis=-1, keepdims=True)
    lifted = jnp.exp(scores - row_top)
    row_mass = jnp.sum(lifted, axis=-1, keepdims=True)
    prob_rows = lifted / row_mass
    prob_low = prob_rows.astype(jnp.bfloat16)
    mixed = jnp.einsum(
        "kgql,lkd->qkgd", prob_low, value_reduced, preferred_element_type=jnp.float32
    )
    attended = mixed.reshape(rows_per_block, QUERY_HEADS * HEAD_WIDTH).astype(jnp.bfloat16)
    branch = back_project(attended, out_wt)
    middle = stream + live_rows * branch
    unit_mid, scale_mid = normalize(middle)
    normed_mid = (unit_mid * ffn_gain).astype(jnp.bfloat16)
    gate_up = apply_projection(normed_mid, gate_up_w)
    gate_pre = gate_up[:, :ff]
    up_pre = gate_up[:, ff:]
    gate_sig = jax.nn.sigmoid(gate_pre)
    gate_act = gate_pre * gate_sig
    hidden = (gate_act * up_pre).astype(jnp.bfloat16)
    grad_out = cotangent.astype(jnp.float32)
    grad_ffn = (live_rows * grad_out).astype(jnp.bfloat16)

    grad_hidden = apply_projection(grad_ffn, down_wt)
    grad_up_pre = (grad_hidden * gate_act).astype(jnp.bfloat16)
    grad_gate_pre = (grad_hidden * up_pre * gate_sig * (1.0 + gate_pre * (1.0 - gate_sig))).astype(
        jnp.bfloat16
    )
    left_mid = both_halves(normed_mid)
    left_ffn = both_halves(grad_ffn)
    owned_down = sum_to_owner(exact(left_ffn, picks[2]), both(hidden), device_count, orders[2])
    owned_gate = sum_to_owner(exact(left_mid, picks[0]), both(grad_gate_pre), device_count, orders[0])
    owned_up = sum_to_owner(exact(left_mid, picks[1]), both(grad_up_pre), device_count, orders[1])

    result = middle + live_rows * back_project(hidden, down_wt)
    grad_mid_norm = back_project(grad_gate_pre, gate_up_w[:, :ff]) + back_project(
        grad_up_pre, gate_up_w[:, ff:]
    )
    grad_ffn_gain = jnp.sum(grad_mid_norm * unit_mid, axis=0)
    grad_middle = grad_out + norm_back(grad_mid_norm * ffn_gain, unit_mid, scale_mid)
    grad_branch = (live_rows * grad_middle).astype(jnp.bfloat16)
    gradient_mixed_values = apply_projection(grad_branch, out_wt).astype(jnp.bfloat16)
    left_branch = both_halves(grad_branch)
    owned_output = sum_to_owner(exact(left_branch, picks[2]), both(attended), device_count, orders[2])
    row_gradient = gradient_mixed_values.reshape(
        rows_per_block, VALUE_HEADS, query_group_width, HEAD_WIDTH
    )
    grad_probs = jnp.einsum(
        "qkgd,lkd->kgql", row_gradient, value_reduced, preferred_element_type=jnp.float32
    )
    centre = jnp.sum(prob_rows * grad_probs, axis=-1, keepdims=True)
    grad_raw = (prob_rows * (grad_probs - centre) * HEAD_WIDTH ** (-0.5)).astype(jnp.bfloat16)
    query_grads = jnp.einsum(
        "kgql,lkd->qkgd", grad_raw, key_rot, preferred_element_type=jnp.float32
    )
    grad_keys = jnp.einsum(
        "kgql,qkgd->lkd", grad_raw, query_rotated, preferred_element_type=jnp.float32
    )
    value_gradient = jnp.einsum(
        "kgql,qkgd->lkd", prob_low, row_gradient, preferred_element_type=jnp.float32
    )
    grad_qrot = query_grads.reshape(token_budget, QUERY_HEADS, HEAD_WIDTH)
    grad_qhead = rotate_back(grad_qrot, cosine_lookup, sine_lookup)
    grad_query_gain = jnp.sum(grad_qhead * query_unit, axis=(0, 1))
    grad_qraw = (
        norm_back(grad_qhead * query_norm_weight, query_unit, query_scale)
        .reshape(token_budget, QUERY_HEADS * HEAD_WIDTH)
        .astype(jnp.bfloat16)
    )
    grad_khead = rotate_back(grad_keys, cosine_lookup, sine_lookup)
    grad_key_gain = jnp.sum(grad_khead * key_unit, axis=(0, 1))
    grad_kraw = (
        norm_back(grad_khead * key_gain, key_unit, key_scale)
        .reshape(token_budget, VALUE_HEADS * HEAD_WIDTH)
        .astype(jnp.bfloat16)
    )
    value_raw_gradient = value_gradient.reshape(token_budget, VALUE_HEADS * HEAD_WIDTH).astype(
        jnp.bfloat16
    )
    left_in = both_halves(rescaled_input)
    owned_query = sum_to_owner(exact(left_in, picks[0]), both(grad_qraw), device_count, orders[0])
    grad_kv = jnp.concatenate([grad_kraw, value_raw_gradient], axis=1)
    owned_kv = sum_to_owner(exact(left_in, picks[1]), both(grad_kv), device_count, orders[1])
    grad_in_norm = back_project(grad_qraw, qkv_w[:, :qw]) + back_project(grad_kv, qkv_w[:, qw:])
    grad_attn_gain = jnp.sum(grad_in_norm * unit_in, axis=0)
    grad_input = grad_middle + norm_back(grad_in_norm * attn_gain, unit_in, scale_in)
    gain_sum = jnp.concatenate(
        [grad_attn_gain, grad_ffn_gain, grad_query_gain, grad_key_gain], axis=0
    ).reshape(device_count, own_gains)
    gain_sum = gain_sum[jnp.arange(device_count, dtype=jnp.int32) ^ me]
    half = device_count
    while half > 1:
        half //= 2
        arrived = swap(gain_sum[half:], device_count, half.bit_length() - 1)
        gain_sum = gain_sum[:half] + arrived
    return (
        result.astype(jnp.bfloat16),
        grad_input,
        owned_query,
        owned_kv[:, :kw],
        owned_kv[:, kw:],
        owned_output.T,
        owned_gate,
        owned_up,
        owned_down.T,
        gain_sum[0],
    )


def solution(mesh):
    in_specs = (
        P("fsdp", None),
        P("fsdp", None),
        P("fsdp", None),
        P("fsdp", None),
        P(None, "fsdp"),
        P("fsdp", None),
        P("fsdp", None),
        P(None, "fsdp"),
        P("fsdp"),
        P("fsdp", None),
        P("fsdp", None),
    )
    out_specs = (
        P("fsdp", None),
        P("fsdp", None),
        P("fsdp", None),
        P("fsdp", None),
        P("fsdp", None),
        P(None, "fsdp"),
        P("fsdp", None),
        P("fsdp", None),
        P(None, "fsdp"),
        P("fsdp"),
    )
    return jax.shard_map(functools.partial(local, mesh.shape["fsdp"]), mesh=mesh, in_specs=in_specs, out_specs=out_specs, check_vma=False)
```

time: 1190 us -> 566 us (0.48)
  waiting for transfers between devices: 845 us -> 320 us
  blocking collectives: 85.8 us -> 0 us
  other arithmetic: 70.5 us -> 38.1 us
  starting transfers between devices: 0.6 us -> 28.6 us
    reduce_scatter x2 -> x0, waiting for transfers between devices: 485 us -> none  [the longest x1 352 us: local(): lax.psum_scatter(jnp.concatenate([contract(normed_mid, grad_gate_pre), co...]
    all_gather x7 -> x1, waiting for transfers between devices: 356 us -> 181 us  [local(): lax.all_gather(jnp.concatenate([w_query, w_key, w_value, w_output.T, w_ga...]
    ppermute x0 -> x39, waiting for transfers between devices: none -> 139 us  [swap(): return lax.ppermute(values, 'fsdp', partners(device_count, bit))]
    unnamed x2 -> x0, blocking collectives: 85.8 us -> none
    concatenate x2 -> x1, other arithmetic: 39.2 us -> 1.07 us  [local(): grad_kv = jnp.concatenate([grad_kraw, value_raw_gradient], axis=1)]
    ppermute x0 -> x39, starting transfers between devices: none -> 28.6 us  [swap(): return lax.ppermute(values, 'fsdp', partners(device_count, bit))]
    dot_general x7 -> x12, matrix products: 36.8 us -> 14 us  [contract(): jnp.einsum('ti,tj->ij', left, right, preferred_element_type=jnp.float32)]
    dot_general x7 -> x4, matrix products: 32.2 us -> 24.5 us  [apply_projection(): return jnp.dot(left, weight, preferred_element_type=jnp.float32)]
  transfers between devices with their start and end apart: 9 -> 40, of which waited for: 9 -> 19; matrix products, arithmetic and copies ran while one was open for 11% -> 9% of each run, Pallas kernels for 0% -> 0%
where the time goes in v1:
time: 566 us; the launch traced here: 560 us
  waiting for transfers between devices  320 us (57%)
  matrix products  111 us (20%)
  local copies, waits for them, and re-layouts  47.1 us (8%)
  other arithmetic  38.1 us (7%)
  starting transfers between devices  28.6 us (5%)
  between operations  16 us (3%)
    all_gather x1, waiting for transfers between devices, local(): lax.all_gather(jnp.concatenate([w_query, w_key, w_value, w_output.T, w_ga...  181 us
    ppermute x39, waiting for transfers between devices, swap(): return lax.ppermute(values, 'fsdp', partners(device_count, bit))  139 us
    dot_general x6, matrix products, back_project(): jnp.einsum('tj,ij->ti', grads, weight, preferred_element_type=jnp.float32)  29.6 us
    ppermute x39, starting transfers between devices, swap(): return lax.ppermute(values, 'fsdp', partners(device_count, bit))  28.6 us
    dot_general x4, matrix products, apply_projection(): return jnp.dot(left, weight, preferred_element_type=jnp.float32)  24.5 us
    unnamed x159, local copies, waits for them, and re-layouts  15 us
    dot_general x12, matrix products, contract(): jnp.einsum('ti,tj->ij', left, right, preferred_element_type=jnp.float32)  14 us
  transfers between devices with their start and end apart: 40, of which 19 were waited for; matrix products, arithmetic and copies ran while one was open for 9% of the time, Pallas kernels for 0%

profile of v1, /device:TPU:0, one launch (start us, length us, event | category | flops | bytes accessed | tf_op | source)
XLA Modules:
  0.0 560.1 jit_solution(16362285775423251489)
XLA Ops:
  23.5 180.8 %all-gather.2.cloned.1.call-done = bf16[1024,15488]{1,0:T(8,128)(2,1)} async-done(((bf16[32,15488]{1,0:T(8,128)(2,1)}), bf16[1024,15488]{1,0:T(8,128)(2,1)}) %all-gather.2.cloned.1.call-update) | async-done | bytes 31719440 | tf_op jit(solution)/shard_map/all_gather | solution.py:161
  206.0 5.8 %fusion.4 = f32[256,4096]{1,0:T(8,128)S(1)} fusion(bf16[1024,15488]{1,0:T(8,128)(2,1)} %all-gather.2.cloned.1.call-done, bf16[256,1024]{1,0:T(8,128)(2,1)S(1)} %copy-done.12, f32[1024]{0:T(1024)S(1)} %get-tuple-element.35, f32[256]{0:T(256)S(1)} %add_rsqrt_fusion.3), kind=kOutput, calls=%fused_computation.5 | convolution fusion | flops 2148532224 | bytes 13112320 | tf_op jit(solution)/shard_map/dot_general | solution.py:61
  214.5 3.1 slice.382
  220.3 2.1 copy.174
  228.1 5.5 fusion.195
  233.6 3.0 convolution_convert_fusion.6
  236.6 4.0 multiply_reduce_fusion.7
  240.8 7.3 %fusion.2 = f32[256,6144]{1,0:T(8,128)S(1)} fusion(bf16[256,1024]{1,0:T(8,128)(2,1)S(1)} %multiply_convert_fusion.5, bf16[1024,15488]{1,0:T(8,128)(2,1)} %all-gather.2.cloned.1.call-done), kind=kOutput, calls=%fused_computation.3 | convolution fusion | flops 3221225472 | bytes 19398656 | tf_op jit(solution)/shard_map/dot_general | solution.py:61
  248.1 7.0 %multiply_convert_fusion.1 = (bf16[256,3072]{1,0:T(8,128)(2,1)S(1)}, bf16[256,3072]{1,0:T(8,128)(2,1)S(1)}, bf16[256,3072]{1,0:T(8,128)(2,1)}) fusion(f32[256,6144]{1,0:T(8,128)S(1)} %fusion.2, bf16[1024,15488]{1,0:T(8,128)(2,1)} %all-gather.2.cloned.1.call-done, bf16[256,1024]{1,0:T(8,128)(2,1)S(1)} %copy-done.10, f32[256]{0:T(256)S(1)} %copy-done.51), kind=kOutput, calls=%fused_computation.41 | convolution fusion | flops 1623195648 | bytes 17826816 | tf_op jit(solution)/shard_map/dot_general | solution.py:61
  255.2 5.9 %fusion.6 = f32[256,1024]{1,0:T(8,128)S(1)} fusion(bf16[256,3072]{1,0:T(8,128)(2,1)S(1)} %get-tuple-element.20, bf16[1024,15488]{1,0:T(8,128)(2,1)} %all-gather.2.cloned.1.call-done), kind=kOutput, calls=%fused_computation.7 | convolution fusion | flops 1610612736 | bytes 8912896 | tf_op jit(solution)/shard_map/tj,ij->ti/dot_general | solution.py:65
  261.1 5.5 multiply_reduce_fusion.4
  268.3 4.4 fusion.27
  272.8 2.3 copy.178
  275.1 4.3 fusion.75
  279.3 2.7 fusion.119
  282.0 9.1 %broadcast_multiply_fusion.1 = (f32[256,8,128]{0,2,1:T(8,128)}, f32[256,8,128]{0,2,1:T(8,128)}) fusion(f32[256,128]{0,1:T(8,128)S(1)} %get-tuple-element.33, bf16[256,8,2,128]{0,3,2,1:T(8,128)(2,1)} %fusion.35, f32[8,256,256,2]{2,1,3,0:T(8,128)} %fusion.119, f32[8,2,256,256]{2,3,1,0:T(8,128)} %get-tuple-element.39, f32[8,2,256]{2,1,0:T(2,128)} %get-tuple-element.38), kind=kOutput, calls=%fused_computation.205 | convolution fusion | flops 276041984 | bytes 11681792 | tf_op jit(solution)/shard_map/kgql,qkgd->lkd/dot_general | solution.py:268
  291.1 9.0 %fusion.49 = f32[8,128,2,256]{3,1,2,0:T(8,128)} fusion(bf16[256,8,128,1]{0,2,3,1:T(8,128)(2,1)} %fusion.104, f32[8,256,256,2]{2,1,3,0:T(8,128)} %fusion.119, f32[8,2,256,256]{2,3,1,0:T(8,128)} %get-tuple-element.39, f32[8,2,256]{2,1,0:T(2,128)} %get-tuple-element.38), kind=kOutput, calls=%fused_computation.89 | convolution fusion | flops 275779840 | bytes 11026432 | tf_op jit(solution)/shard_map/kgql,lkd->qkgd/dot_general | solution.py:265
  300.1 3.2 copy.150
  305.1 2.6 fusion.190
  307.7 3.5 copy.153
  311.2 3.5 copy.152
  314.7 4.2 pad_maximum_fusion.3
  323.2 2.9 copy.155
  326.1 3.1 multiply_reduce_fusion
  333.6 5.3 fusion.32
  340.9 3.5 fusion.14
  344.6 5.1 fusion.90
  352.1 2.9 fusion.89
  354.9 5.6 fusion.72
  362.3 2.6 collective-permute-done.35
  378.8 2.4 convolution_convert_fusion.5
  390.6 16.6 %collective-permute-done.2 = bf16[256,2048]{1,0:T(8,128)(2,1)S(1)} collective-permute-done((bf16[256,2048]{1,0:T(8,128)(2,1)S(1)}, bf16[256,2048]{1,0:T(8,128)(2,1)S(1)}, u32[]{:S(2)}, u32[]{:S(2)}) %collective-permute-start.2) | collective-permute-done | bytes 1048608 | tf_op jit(solution)/shard_map/ppermute | solution.py:131
  407.7 2.3 convolution_add_fusion.5
  413.9 39.3 %collective-permute-done.3 = bf16[128,2048]{1,0:T(8,128)(2,1)S(1)} collective-permute-done((bf16[128,2048]{1,0:T(8,128)(2,1)S(1)}, bf16[128,2048]{1,0:T(8,128)(2,1)S(1)}, u32[]{:S(2)}, u32[]{:S(2)}) %collective-permute-start.3) | collective-permute-done | bytes 524320 | tf_op jit(solution)/shard_map/ppermute | solution.py:131
  454.8 11.2 %collective-permute-done.14 = bf16[128,2048]{1,0:T(8,128)(2,1)S(1)} collective-permute-done((bf16[128,2048]{1,0:T(8,128)(2,1)S(1)}, bf16[128,2048]{1,0:T(8,128)(2,1)S(1)}, u32[]{:S(2)}, u32[]{:S(2)}) %collective-permute-start.14) | collective-permute-done | bytes 524320 | tf_op jit(solution)/shard_map/ppermute | solution.py:131
  467.6 4.8 collective-permute-done.9
  472.4 1.9 collective-permute-start.5
  475.5 8.4 %collective-permute-done.5 = bf16[32,2048]{1,0:T(8,128)(2,1)S(1)} collective-permute-done((bf16[32,2048]{1,0:T(8,128)(2,1)S(1)}, bf16[32,2048]{1,0:T(8,128)(2,1)S(1)}, u32[]{:S(2)}, u32[]{:S(2)}) %collective-permute-start.5) | collective-permute-done | bytes 131104 | tf_op jit(solution)/shard_map/ppermute | solution.py:131
  484.6 2.1 collective-permute-done.10
  486.8 3.0 collective-permute-done.16
  497.9 11.5 %collective-permute-done.20 = bf16[128,3072]{1,0:T(8,128)(2,1)S(1)} collective-permute-done((bf16[128,3072]{1,0:T(8,128)(2,1)S(1)}, bf16[128,3072]{1,0:T(8,128)(2,1)S(1)}, u32[]{:S(2)}, u32[]{:S(2)}) %collective-permute-start.20) | collective-permute-done | bytes 786464 | tf_op jit(solution)/shard_map/ppermute | solution.py:131
  509.7 5.4 collective-permute-done.25
  515.4 13.5 %collective-permute-done.31 = bf16[128,3072]{1,0:T(8,128)(2,1)S(1)} collective-permute-done((bf16[128,3072]{1,0:T(8,128)(2,1)S(1)}, bf16[128,3072]{1,0:T(8,128)(2,1)S(1)}, u32[]{:S(2)}, u32[]{:S(2)}) %collective-permute-start.31) | collective-permute-done | bytes 786464 | tf_op jit(solution)/shard_map/ppermute | solution.py:131
  530.8 3.0 collective-permute-start.27
  533.8 3.5 collective-permute-done.32
  537.5 7.3 %collective-permute-done.22 = bf16[32,3072]{1,0:T(8,128)(2,1)S(1)} collective-permute-done((bf16[32,3072]{1,0:T(8,128)(2,1)S(1)}, bf16[32,3072]{1,0:T(8,128)(2,1)S(1)}, u32[]{:S(2)}, u32[]{:S(2)}) %collective-permute-start.22) | collective-permute-done | bytes 196640 | tf_op jit(solution)/shard_map/ppermute | solution.py:131
  545.5 3.4 collective-permute-done.27
  549.7 2.3 collective-permute-done.33
  (355 shorter events, 92.5 us)
Async XLA Ops:
  7.2 8.2 %copy-start.72 = (s32[1,4]{1,0:T(1,128)S(1)}, s32[1,4]{1,0:T(1,128)}, u32[]{:S(2)}) copy-start(s32[1,4]{1,0:T(1,128)} %param.20) | copy-start | bytes 52
  7.2 9.0 %copy-start.9 = (bf16[256,1024]{1,0:T(8,128)(2,1)S(1)}, bf16[256,1024]{1,0:T(8,128)(2,1)}, u32[]{:S(2)}) copy-start(bf16[256,1024]{1,0:T(8,128)(2,1)} %param.21) | copy-start | bytes 1572868
  7.2 197.1 %all-gather.2.cloned.1.call-start = ((), (), s32[]{:S(2)}) async-start(), calls=%async_computation | async-start | bytes 32710656 | tf_op jit(solution)/shard_map/all_gather | solution.py:161
  11.8 8.0 %copy-start.12 = (bf16[256,1024]{1,0:T(8,128)(2,1)S(1)}, bf16[256,1024]{1,0:T(8,128)(2,1)}, u32[]{:S(2)}) copy-start(bf16[256,1024]{1,0:T(8,128)(2,1)} %param.11) | copy-start | bytes 1572868
  16.8 5.4 collective-permute-start.28
  19.9 186.1 %copy-start.53 = (f32[256]{0:T(256)}, f32[256]{0:T(256)S(1)}, u32[]{:S(2)}) copy-start(f32[256]{0:T(256)S(1)} %add_rsqrt_fusion.3) | copy-start | bytes 3076
  240.6 26.0 %copy-start = (f32[256,1024]{1,0:T(8,128)}, f32[256,1024]{1,0:T(8,128)S(1)}, u32[]{:S(2)}) copy-start(f32[256,1024]{1,0:T(8,128)S(1)} %get-tuple-element.41) | copy-start | bytes 3145732
  240.6 26.0 %copy-start.39 = (f32[256]{0:T(256)}, f32[256]{0:T(256)S(1)}, u32[]{:S(2)}) copy-start(f32[256]{0:T(256)S(1)} %add_rsqrt_fusion.2) | copy-start | bytes 3076
  338.8 39.0 %collective-permute-start.1 = (bf16[256,2048]{1,0:T(8,128)(2,1)}, bf16[256,2048]{1,0:T(8,128)(2,1)}, u32[]{:S(2)}, u32[]{:S(2)}) collective-permute-start(bf16[256,2048]{1,0:T(8,128)(2,1)} %fusion.32), channel_id=1, source_target_pairs={{0,1},{1,0},{2,3},{3,2},{4,5},{5,4},{6,7},{7,6},{8,9},{9,8},{10,11... | collective-permute-start | bytes 3145736 | tf_op jit(solution)/shard_map/ppermute | solution.py:131
  350.5 10.7 %collective-permute-start.34 = (f32[16,72]{1,0:T(8,128)S(1)}, f32[16,72]{1,0:T(8,128)S(1)}, u32[]{:S(2)}, u32[]{:S(2)}) collective-permute-start(f32[16,72]{1,0:T(8,128)S(1)} %slice.451), channel_id=1, source_target_pairs={{0,16},{1,17},{2,18},{3,19},{4,20},{5,21},{6,22},{7,23},{8,24},{9,... | collective-permute-start | bytes 13832 | tf_op jit(solution)/shard_map/ppermute | solution.py:131
  361.2 8.6 %copy-start.31 = (bf16[256,1024]{1,0:T(8,128)(2,1)S(1)}, bf16[256,1024]{1,0:T(8,128)(2,1)}, u32[]{:S(2)}) copy-start(bf16[256,1024]{1,0:T(8,128)(2,1)} %copy-done.30) | copy-start | bytes 1572868
  361.2 3.7 collective-permute-start.35
  362.3 8.0 %copy-start.71 = (bf16[256,512]{1,0:T(8,128)(2,1)S(1)}, bf16[256,512]{1,0:T(8,128)(2,1)}, u32[]{:S(2)}) copy-start(bf16[256,512]{1,0:T(8,128)(2,1)} %fusion.80) | copy-start | bytes 786436
  364.9 3.6 collective-permute-start.36
  366.9 17.9 %collective-permute-start.18 = (bf16[256,3072]{1,0:T(8,128)(2,1)S(1)}, bf16[256,3072]{1,0:T(8,128)(2,1)S(1)}, u32[]{:S(2)}, u32[]{:S(2)}) collective-permute-start(bf16[256,3072]{1,0:T(8,128)(2,1)S(1)} %copy-done.68), channel_id=1, source_target_pairs={{0,1},{1,0},{2,3},{3,2},{4,5},{5,4},{6,7},{7,6},{8,9},{9,8},{10,11... | collective-permute-start | bytes 4718600 | tf_op jit(solution)/shard_map/ppermute | solution.py:131
  368.5 3.6 collective-permute-start.37
  370.3 3.8 collective-permute-start
  372.1 1.2 collective-permute-start.38
  372.6 8.5 %collective-permute-start.6 = (bf16[256,2048]{0,1:T(8,128)(2,1)S(1)}, bf16[256,2048]{0,1:T(8,128)(2,1)S(1)}, u32[]{:S(2)}, u32[]{:S(2)}) collective-permute-start(bf16[256,2048]{0,1:T(8,128)(2,1)S(1)} %copy-done.23), channel_id=1, source_target_pairs={{0,1},{1,0},{2,3},{3,2},{4,5},{5,4},{6,7},{7,6},{8,9},{9,8},{10,11... | collective-permute-start | bytes 3145736 | tf_op jit(solution)/shard_map/ppermute | solution.py:131
  373.2 3.9 collective-permute-start.11
  374.1 2.1 collective-permute-start.17
  376.3 7.0 %collective-permute-start.12 = (bf16[256,2048]{0,1:T(8,128)(2,1)S(1)}, bf16[256,2048]{0,1:T(8,128)(2,1)S(1)}, u32[]{:S(2)}, u32[]{:S(2)}) collective-permute-start(bf16[256,2048]{0,1:T(8,128)(2,1)S(1)} %bitcast.192), channel_id=1, source_target_pairs={{0,1},{1,0},{2,3},{3,2},{4,5},{5,4},{6,7},{7,6},{8,9},{9,8},{10,11... | collective-permute-start | bytes 3145736 | tf_op jit(solution)/shard_map/ppermute | solution.py:131
  377.1 9.3 %collective-permute-start.23 = (bf16[256,3072]{1,0:T(8,128)(2,1)S(1)}, bf16[256,3072]{1,0:T(8,128)(2,1)S(1)}, u32[]{:S(2)}, u32[]{:S(2)}) collective-permute-start(bf16[256,3072]{1,0:T(8,128)(2,1)S(1)} %copy-done.66), channel_id=1, source_target_pairs={{0,1},{1,0},{2,3},{3,2},{4,5},{5,4},{6,7},{7,6},{8,9},{9,8},{10,11... | collective-permute-start | bytes 4718600 | tf_op jit(solution)/shard_map/ppermute | solution.py:131
  377.8 11.1 %collective-permute-start.29 = (bf16[256,3072]{1,0:T(8,128)(2,1)S(1)}, bf16[256,3072]{1,0:T(8,128)(2,1)S(1)}, u32[]{:S(2)}, u32[]{:S(2)}) collective-permute-start(bf16[256,3072]{1,0:T(8,128)(2,1)S(1)} %copy-done.64), channel_id=1, source_target_pairs={{0,1},{1,0},{2,3},{3,2},{4,5},{5,4},{6,7},{7,6},{8,9},{9,8},{10,11... | collective-permute-start | bytes 4718600 | tf_op jit(solution)/shard_map/ppermute | solution.py:131
  381.2 26.1 %collective-permute-start.2 = (bf16[256,2048]{1,0:T(8,128)(2,1)S(1)}, bf16[256,2048]{1,0:T(8,128)(2,1)S(1)}, u32[]{:S(2)}, u32[]{:S(2)}) collective-permute-start(bf16[256,2048]{1,0:T(8,128)(2,1)S(1)} %convolution_convert_fusion.5), channel_id=1, source_target_pairs={{0,2},{1,3},{2,0},{3,1},{4,6},{5,7},{6,4},{7,5},{8,10},{9,11},{10,... | collective-permute-start | bytes 3145736 | tf_op jit(solution)/shard_map/ppermute | solution.py:131
  383.3 26.8 %collective-permute-start.7 = (bf16[256,2048]{1,0:T(8,128)(2,1)S(1)}, bf16[256,2048]{1,0:T(8,128)(2,1)S(1)}, u32[]{:S(2)}, u32[]{:S(2)}) collective-permute-start(bf16[256,2048]{1,0:T(8,128)(2,1)S(1)} %convolution_convert_fusion.4), channel_id=1, source_target_pairs={{0,4},{1,5},{2,6},{3,7},{4,0},{5,1},{6,2},{7,3},{8,12},{9,13},{10,... | collective-permute-start | bytes 3145736 | tf_op jit(solution)/shard_map/ppermute | solution.py:131
  384.9 27.6 %collective-permute-start.13 = (bf16[256,2048]{1,0:T(8,128)(2,1)S(1)}, bf16[256,2048]{1,0:T(8,128)(2,1)S(1)}, u32[]{:S(2)}, u32[]{:S(2)}) collective-permute-start(bf16[256,2048]{1,0:T(8,128)(2,1)S(1)} %convolution_convert_fusion.3), channel_id=1, source_target_pairs={{0,8},{1,9},{2,10},{3,11},{4,12},{5,13},{6,14},{7,15},{8,0},{9,1},... | collective-permute-start | bytes 3145736 | tf_op jit(solution)/shard_map/ppermute | solution.py:131
  386.5 104.1 %collective-permute-start.19 = (bf16[256,3072]{1,0:T(8,128)(2,1)S(1)}, bf16[256,3072]{1,0:T(8,128)(2,1)S(1)}, u32[]{:S(2)}, u32[]{:S(2)}) collective-permute-start(bf16[256,3072]{1,0:T(8,128)(2,1)S(1)} %convolution_convert_fusion.2), channel_id=1, source_target_pairs={{0,2},{1,3},{2,0},{3,1},{4,6},{5,7},{6,4},{7,5},{8,10},{9,11},{10,... | collective-permute-start | bytes 4718600 | tf_op jit(solution)/shard_map/ppermute | solution.py:131
  389.0 104.2 %collective-permute-start.24 = (bf16[256,3072]{1,0:T(8,128)(2,1)S(1)}, bf16[256,3072]{1,0:T(8,128)(2,1)S(1)}, u32[]{:S(2)}, u32[]{:S(2)}) collective-permute-start(bf16[256,3072]{1,0:T(8,128)(2,1)S(1)} %convolution_convert_fusion.1), channel_id=1, source_target_pairs={{0,4},{1,5},{2,6},{3,7},{4,0},{5,1},{6,2},{7,3},{8,12},{9,13},{10,... | collective-permute-start | bytes 4718600 | tf_op jit(solution)/shard_map/ppermute | solution.py:131
  407.3 88.9 %collective-permute-start.30 = (bf16[256,3072]{1,0:T(8,128)(2,1)S(1)}, bf16[256,3072]{1,0:T(8,128)(2,1)S(1)}, u32[]{:S(2)}, u32[]{:S(2)}) collective-permute-start(bf16[256,3072]{1,0:T(8,128)(2,1)S(1)} %convolution_convert_fusion), channel_id=1, source_target_pairs={{0,8},{1,9},{2,10},{3,11},{4,12},{5,13},{6,14},{7,15},{8,0},{9,1},... | collective-permute-start | bytes 4718600 | tf_op jit(solution)/shard_map/ppermute | solution.py:131
  410.1 43.1 %collective-permute-start.3 = (bf16[128,2048]{1,0:T(8,128)(2,1)S(1)}, bf16[128,2048]{1,0:T(8,128)(2,1)S(1)}, u32[]{:S(2)}, u32[]{:S(2)}) collective-permute-start(bf16[128,2048]{1,0:T(8,128)(2,1)S(1)} %slice.584), channel_id=1, source_target_pairs={{0,4},{1,5},{2,6},{3,7},{4,0},{5,1},{6,2},{7,3},{8,12},{9,13},{10,... | collective-permute-start | bytes 1572872 | tf_op jit(solution)/shard_map/ppermute | solution.py:131
  412.5 41.7 %collective-permute-start.8 = (bf16[128,2048]{1,0:T(8,128)(2,1)S(1)}, bf16[128,2048]{1,0:T(8,128)(2,1)S(1)}, u32[]{:S(2)}, u32[]{:S(2)}) collective-permute-start(bf16[128,2048]{1,0:T(8,128)(2,1)S(1)} %slice.583), channel_id=1, source_target_pairs={{0,2},{1,3},{2,0},{3,1},{4,6},{5,7},{6,4},{7,5},{8,10},{9,11},{10,... | collective-permute-start | bytes 1572872 | tf_op jit(solution)/shard_map/ppermute | solution.py:131
  453.2 12.8 %collective-permute-start.14 = (bf16[128,2048]{1,0:T(8,128)(2,1)S(1)}, bf16[128,2048]{1,0:T(8,128)(2,1)S(1)}, u32[]{:S(2)}, u32[]{:S(2)}) collective-permute-start(bf16[128,2048]{1,0:T(8,128)(2,1)S(1)} %slice.582), channel_id=1, source_target_pairs={{0,2},{1,3},{2,0},{3,1},{4,6},{5,7},{6,4},{7,5},{8,10},{9,11},{10,... | collective-permute-start | bytes 1572872 | tf_op jit(solution)/shard_map/ppermute | solution.py:131
  454.1 12.5 %collective-permute-start.4 = (bf16[64,2048]{1,0:T(8,128)(2,1)S(1)}, bf16[64,2048]{1,0:T(8,128)(2,1)S(1)}, u32[]{:S(2)}, u32[]{:S(2)}) collective-permute-start(bf16[64,2048]{1,0:T(8,128)(2,1)S(1)} %slice.590), channel_id=1, source_target_pairs={{0,8},{1,9},{2,10},{3,11},{4,12},{5,13},{6,14},{7,15},{8,0},{9,1},... | collective-permute-start | bytes 786440 | tf_op jit(solution)/shard_map/ppermute | solution.py:131
  466.0 6.4 %collective-permute-start.9 = (bf16[64,2048]{1,0:T(8,128)(2,1)S(1)}, bf16[64,2048]{1,0:T(8,128)(2,1)S(1)}, u32[]{:S(2)}, u32[]{:S(2)}) collective-permute-start(bf16[64,2048]{1,0:T(8,128)(2,1)S(1)} %slice.589), channel_id=1, source_target_pairs={{0,8},{1,9},{2,10},{3,11},{4,12},{5,13},{6,14},{7,15},{8,0},{9,1},... | collective-permute-start | bytes 786440 | tf_op jit(solution)/shard_map/ppermute | solution.py:131
  466.6 7.8 %collective-permute-start.15 = (bf16[64,2048]{1,0:T(8,128)(2,1)S(1)}, bf16[64,2048]{1,0:T(8,128)(2,1)S(1)}, u32[]{:S(2)}, u32[]{:S(2)}) collective-permute-start(bf16[64,2048]{1,0:T(8,128)(2,1)S(1)} %slice.588), channel_id=1, source_target_pairs={{0,4},{1,5},{2,6},{3,7},{4,0},{5,1},{6,2},{7,3},{8,12},{9,13},{10,... | collective-permute-start | bytes 786440 | tf_op jit(solution)/shard_map/ppermute | solution.py:131
  472.4 11.5 %collective-permute-start.5 = (bf16[32,2048]{1,0:T(8,128)(2,1)S(1)}, bf16[32,2048]{1,0:T(8,128)(2,1)S(1)}, u32[]{:S(2)}, u32[]{:S(2)}) collective-permute-start(bf16[32,2048]{1,0:T(8,128)(2,1)S(1)} %slice.596), channel_id=1, source_target_pairs={{0,16},{1,17},{2,18},{3,19},{4,20},{5,21},{6,22},{7,23},{8,24},{9,... | collective-permute-start | bytes 393224 | tf_op jit(solution)/shard_map/ppermute | solution.py:131
  474.4 12.3 %collective-permute-start.10 = (bf16[32,2048]{1,0:T(8,128)(2,1)S(1)}, bf16[32,2048]{1,0:T(8,128)(2,1)S(1)}, u32[]{:S(2)}, u32[]{:S(2)}) collective-permute-start(bf16[32,2048]{1,0:T(8,128)(2,1)S(1)} %slice.595), channel_id=1, source_target_pairs={{0,16},{1,17},{2,18},{3,19},{4,20},{5,21},{6,22},{7,23},{8,24},{9,... | collective-permute-start | bytes 393224 | tf_op jit(solution)/shard_map/ppermute | solution.py:131
  483.9 5.9 %collective-permute-start.16 = (bf16[32,2048]{1,0:T(8,128)(2,1)S(1)}, bf16[32,2048]{1,0:T(8,128)(2,1)S(1)}, u32[]{:S(2)}, u32[]{:S(2)}) collective-permute-start(bf16[32,2048]{1,0:T(8,128)(2,1)S(1)} %slice.594), channel_id=1, source_target_pairs={{0,16},{1,17},{2,18},{3,19},{4,20},{5,21},{6,22},{7,23},{8,24},{9,... | collective-permute-start | bytes 393224 | tf_op jit(solution)/shard_map/ppermute | solution.py:131
  491.6 17.8 %collective-permute-start.20 = (bf16[128,3072]{1,0:T(8,128)(2,1)S(1)}, bf16[128,3072]{1,0:T(8,128)(2,1)S(1)}, u32[]{:S(2)}, u32[]{:S(2)}) collective-permute-start(bf16[128,3072]{1,0:T(8,128)(2,1)S(1)} %slice.581), channel_id=1, source_target_pairs={{0,4},{1,5},{2,6},{3,7},{4,0},{5,1},{6,2},{7,3},{8,12},{9,13},{10,... | collective-permute-start | bytes 2359304 | tf_op jit(solution)/shard_map/ppermute | solution.py:131
  494.6 20.5 %collective-permute-start.25 = (bf16[128,3072]{1,0:T(8,128)(2,1)S(1)}, bf16[128,3072]{1,0:T(8,128)(2,1)S(1)}, u32[]{:S(2)}, u32[]{:S(2)}) collective-permute-start(bf16[128,3072]{1,0:T(8,128)(2,1)S(1)} %slice.580), channel_id=1, source_target_pairs={{0,2},{1,3},{2,0},{3,1},{4,6},{5,7},{6,4},{7,5},{8,10},{9,11},{10,... | collective-permute-start | bytes 2359304 | tf_op jit(solution)/shard_map/ppermute | solution.py:131
  497.2 31.7 %collective-permute-start.31 = (bf16[128,3072]{1,0:T(8,128)(2,1)S(1)}, bf16[128,3072]{1,0:T(8,128)(2,1)S(1)}, u32[]{:S(2)}, u32[]{:S(2)}) collective-permute-start(bf16[128,3072]{1,0:T(8,128)(2,1)S(1)} %slice.579), channel_id=1, source_target_pairs={{0,2},{1,3},{2,0},{3,1},{4,6},{5,7},{6,4},{7,5},{8,10},{9,11},{10,... | collective-permute-start | bytes 2359304 | tf_op jit(solution)/shard_map/ppermute | solution.py:131
  509.6 20.9 %collective-permute-start.21 = (bf16[64,3072]{1,0:T(8,128)(2,1)S(1)}, bf16[64,3072]{1,0:T(8,128)(2,1)S(1)}, u32[]{:S(2)}, u32[]{:S(2)}) collective-permute-start(bf16[64,3072]{1,0:T(8,128)(2,1)S(1)} %slice.587), channel_id=1, source_target_pairs={{0,8},{1,9},{2,10},{3,11},{4,12},{5,13},{6,14},{7,15},{8,0},{9,1},... | collective-permute-start | bytes 1179656 | tf_op jit(solution)/shard_map/ppermute | solution.py:131
  515.4 15.3 %collective-permute-start.26 = (bf16[64,3072]{1,0:T(8,128)(2,1)S(1)}, bf16[64,3072]{1,0:T(8,128)(2,1)S(1)}, u32[]{:S(2)}, u32[]{:S(2)}) collective-permute-start(bf16[64,3072]{1,0:T(8,128)(2,1)S(1)} %slice.586), channel_id=1, source_target_pairs={{0,8},{1,9},{2,10},{3,11},{4,12},{5,13},{6,14},{7,15},{8,0},{9,1},... | collective-permute-start | bytes 1179656 | tf_op jit(solution)/shard_map/ppermute | solution.py:131
  529.2 8.1 %collective-permute-start.32 = (bf16[64,3072]{1,0:T(8,128)(2,1)S(1)}, bf16[64,3072]{1,0:T(8,128)(2,1)S(1)}, u32[]{:S(2)}, u32[]{:S(2)}) collective-permute-start(bf16[64,3072]{1,0:T(8,128)(2,1)S(1)} %slice.585), channel_id=1, source_target_pairs={{0,4},{1,5},{2,6},{3,7},{4,0},{5,1},{6,2},{7,3},{8,12},{9,13},{10,... | collective-permute-start | bytes 1179656 | tf_op jit(solution)/shard_map/ppermute | solution.py:131
  530.6 14.1 %collective-permute-start.22 = (bf16[32,3072]{1,0:T(8,128)(2,1)S(1)}, bf16[32,3072]{1,0:T(8,128)(2,1)S(1)}, u32[]{:S(2)}, u32[]{:S(2)}) collective-permute-start(bf16[32,3072]{1,0:T(8,128)(2,1)S(1)} %slice.593), channel_id=1, source_target_pairs={{0,16},{1,17},{2,18},{3,19},{4,20},{5,21},{6,22},{7,23},{8,24},{9,... | collective-permute-start | bytes 589832 | tf_op jit(solution)/shard_map/ppermute | solution.py:131
  530.8 18.2 %collective-permute-start.27 = (bf16[32,3072]{1,0:T(8,128)(2,1)S(1)}, bf16[32,3072]{1,0:T(8,128)(2,1)S(1)}, u32[]{:S(2)}, u32[]{:S(2)}) collective-permute-start(bf16[32,3072]{1,0:T(8,128)(2,1)S(1)} %slice.592), channel_id=1, source_target_pairs={{0,16},{1,17},{2,18},{3,19},{4,20},{5,21},{6,22},{7,23},{8,24},{9,... | collective-permute-start | bytes 589832 | tf_op jit(solution)/shard_map/ppermute | solution.py:131
  537.4 14.7 %collective-permute-start.33 = (bf16[32,3072]{1,0:T(8,128)(2,1)S(1)}, bf16[32,3072]{1,0:T(8,128)(2,1)S(1)}, u32[]{:S(2)}, u32[]{:S(2)}) collective-permute-start(bf16[32,3072]{1,0:T(8,128)(2,1)S(1)} %slice.591), channel_id=1, source_target_pairs={{0,16},{1,17},{2,18},{3,19},{4,20},{5,21},{6,22},{7,23},{8,24},{9,... | collective-permute-start | bytes 589832 | tf_op jit(solution)/shard_map/ppermute | solution.py:131
  (66 other events, 249.2 us)
Sparse Core Ops, SparseCore 0:
  15.5 188.7 all-gather.1

commit v2 on v1

--- a/solution.py
+++ b/solution.py
@@ -131,16 +131,42 @@
     return lax.ppermute(values, "fsdp", partners(device_count, bit))
 
 
-def sum_to_owner(left, right, device_count, order):
-    half = left.shape[1] // 2
-    sent = contract(left[:, half:], right).astype(jnp.bfloat16)
-    arrived = swap(sent, device_count, order[0])
-    total = contract(left[:, :half], right) + arrived.astype(jnp.float32)
-    for bit in order[1:]:
-        half //= 2
-        arrived = swap(total[half:].astype(jnp.bfloat16), device_count, bit)
-        total = total[:half] + arrived.astype(jnp.float32)
-    return total
+class OwnerSum:
+    def __init__(self, left, right, device_count, order):
+        self.device_count, self.order = device_count, order
+        half = left.shape[1] // 2
+        sent = contract(left[:, half:], right).astype(jnp.bfloat16)
+        self.arrived = swap(sent, device_count, order[0])
+        self.kept = contract(left[:, :half], right)
+        self.step = 1
+
+    def advance(self):
+        if self.arrived is None:
+            return
+        total = self.kept + self.arrived.astype(jnp.float32)
+        if self.step == len(self.order):
+            self.kept, self.arrived = total, None
+            return
+        half = total.shape[0] // 2
+        self.arrived = swap(
+            total[half:].astype(jnp.bfloat16), self.device_count, self.order[self.step]
+        )
+        self.kept = total[:half]
+        self.step += 1
+
+    def finish(self):
+        while self.arrived is not None:
+            self.advance()
+        return self.kept
+
+
+def after(values, sums):
+    going = [one for one in sums if one.arrived is not None]
+    values, landed = lax.optimization_barrier((values, [one.arrived for one in going]))
+    for one, arrived in zip(going, landed):
+        one.arrived = arrived
+        one.advance()
+    return values
 
 
 def local(
@@ -240,20 +266,28 @@
     )
     left_mid = both_halves(normed_mid)
     left_ffn = both_halves(grad_ffn)
-    owned_down = sum_to_owner(exact(left_ffn, picks[2]), both(hidden), device_count, orders[2])
-    owned_gate = sum_to_owner(exact(left_mid, picks[0]), both(grad_gate_pre), device_count, orders[0])
-    owned_up = sum_to_owner(exact(left_mid, picks[1]), both(grad_up_pre), device_count, orders[1])
+    exchanged = (left_mid, left_ffn, both(hidden), both(grad_gate_pre), both(grad_up_pre))
 
     result = middle + live_rows * back_project(hidden, down_wt)
     grad_mid_norm = back_project(grad_gate_pre, gate_up_w[:, :ff]) + back_project(
         grad_up_pre, gate_up_w[:, ff:]
     )
+    (grad_mid_norm, result), exchanged = lax.optimization_barrier(
+        ((grad_mid_norm, result), exchanged)
+    )
+    left_mid, left_ffn, both_hidden, both_gate, both_up = exchanged
+    sums = [
+        OwnerSum(exact(left_mid, picks[0]), both_gate, device_count, orders[0]),
+        OwnerSum(exact(left_mid, picks[1]), both_up, device_count, orders[1]),
+        OwnerSum(exact(left_ffn, picks[2]), both_hidden, device_count, orders[2]),
+    ]
     grad_ffn_gain = jnp.sum(grad_mid_norm * unit_mid, axis=0)
     grad_middle = grad_out + norm_back(grad_mid_norm * ffn_gain, unit_mid, scale_mid)
     grad_branch = (live_rows * grad_middle).astype(jnp.bfloat16)
     gradient_mixed_values = apply_projection(grad_branch, out_wt).astype(jnp.bfloat16)
     left_branch = both_halves(grad_branch)
-    owned_output = sum_to_owner(exact(left_branch, picks[2]), both(attended), device_count, orders[2])
+    both_attended = both(attended)
+    left_in = both_halves(rescaled_input)
     row_gradient = gradient_mixed_values.reshape(
         rows_per_block, VALUE_HEADS, query_group_width, HEAD_WIDTH
     )
@@ -262,6 +296,10 @@
     )
     centre = jnp.sum(prob_rows * grad_probs, axis=-1, keepdims=True)
     grad_raw = (prob_rows * (grad_probs - centre) * HEAD_WIDTH ** (-0.5)).astype(jnp.bfloat16)
+    grad_raw, left_branch, both_attended, left_in = after(
+        (grad_raw, left_branch, both_attended, left_in), sums
+    )
+    sums.append(OwnerSum(exact(left_branch, picks[2]), both_attended, device_count, orders[2]))
     query_grads = jnp.einsum(
         "kgql,lkd->qkgd", grad_raw, key_rot, preferred_element_type=jnp.float32
     )
@@ -271,6 +309,19 @@
     value_gradient = jnp.einsum(
         "kgql,qkgd->lkd", prob_low, row_gradient, preferred_element_type=jnp.float32
     )
+    query_grads, grad_keys, value_gradient = after((query_grads, grad_keys, value_gradient), sums)
+    grad_khead = rotate_back(grad_keys, cosine_lookup, sine_lookup)
+    grad_key_gain = jnp.sum(grad_khead * key_unit, axis=(0, 1))
+    grad_kraw = (
+        norm_back(grad_khead * key_gain, key_unit, key_scale)
+        .reshape(token_budget, VALUE_HEADS * HEAD_WIDTH)
+        .astype(jnp.bfloat16)
+    )
+    value_raw_gradient = value_gradient.reshape(token_budget, VALUE_HEADS * HEAD_WIDTH).astype(
+        jnp.bfloat16
+    )
+    grad_kv = jnp.concatenate([grad_kraw, value_raw_gradient], axis=1)
+    both_kv = both(grad_kv)
     grad_qrot = query_grads.reshape(token_budget, QUERY_HEADS, HEAD_WIDTH)
     grad_qhead = rotate_back(grad_qrot, cosine_lookup, sine_lookup)
     grad_query_gain = jnp.sum(grad_qhead * query_unit, axis=(0, 1))
@@ -279,23 +330,18 @@
         .reshape(token_budget, QUERY_HEADS * HEAD_WIDTH)
         .astype(jnp.bfloat16)
     )
-    grad_khead = rotate_back(grad_keys, cosine_lookup, sine_lookup)
-    grad_key_gain = jnp.sum(grad_khead * key_unit, axis=(0, 1))
-    grad_kraw = (
-        norm_back(grad_khead * key_gain, key_unit, key_scale)
-        .reshape(token_budget, VALUE_HEADS * HEAD_WIDTH)
-        .astype(jnp.bfloat16)
-    )
-    value_raw_gradient = value_gradient.reshape(token_budget, VALUE_HEADS * HEAD_WIDTH).astype(
-        jnp.bfloat16
-    )
-    left_in = both_halves(rescaled_input)
-    owned_query = sum_to_owner(exact(left_in, picks[0]), both(grad_qraw), device_count, orders[0])
-    grad_kv = jnp.concatenate([grad_kraw, value_raw_gradient], axis=1)
-    owned_kv = sum_to_owner(exact(left_in, picks[1]), both(grad_kv), device_count, orders[1])
-    grad_in_norm = back_project(grad_qraw, qkv_w[:, :qw]) + back_project(grad_kv, qkv_w[:, qw:])
+    grad_qraw, both_kv = after((grad_qraw, both_kv), sums)
+    sums.append(OwnerSum(exact(left_in, picks[1]), both_kv, device_count, orders[1]))
+    both_query = both(grad_qraw)
+    grad_in_kv = back_project(grad_kv, qkv_w[:, qw:])
+    both_query, grad_in_kv = lax.optimization_barrier((both_query, grad_in_kv))
+    sums.append(OwnerSum(exact(left_in, picks[0]), both_query, device_count, orders[0]))
+    grad_in_norm = back_project(grad_qraw, qkv_w[:, :qw]) + grad_in_kv
     grad_attn_gain = jnp.sum(grad_in_norm * unit_in, axis=0)
     grad_input = grad_middle + norm_back(grad_in_norm * attn_gain, unit_in, scale_in)
+    owned_gate, owned_up, owned_down, owned_output, owned_kv, owned_query = [
+        one.finish() for one in sums
+    ]
     gain_sum = jnp.concatenate(
         [grad_attn_gain, grad_ffn_gain, grad_query_gain, grad_key_gain], axis=0
     ).reshape(device_count, own_gains)

time: 566 us -> 570 us (level)
  waiting for transfers between devices: 320 us -> 295 us
  other arithmetic: 38.1 us -> 60.9 us
  local copies, waits for them, and re-layouts: 47.1 us -> 58 us
  matrix products: 111 us -> 105 us
    ppermute x39, waiting for transfers between devices: 139 us -> 114 us  [swap(): return lax.ppermute(values, 'fsdp', partners(device_count, bit))]
    concatenate x0 -> x10, other arithmetic: none -> 18.4 us  [the longest x6 14.7 us: both(): return jnp.concatenate([values, swap(values, device_count, 0)], axis=0)]
    dot_general x12, matrix products: 14 us -> 21.4 us  [contract(): jnp.einsum('ti,tj->ij', left, right, preferred_element_type=jnp.float32)]
    dot_general x1, matrix products: 9.09 us -> 1.79 us  [local(): jnp.einsum('kgql,qkgd->lkd', grad_raw, query_rotated, preferred_element_t...]
    dot_general x1, matrix products: 8.98 us -> 1.81 us  [local(): jnp.einsum('kgql,lkd->qkgd', grad_raw, key_rot, preferred_element_type=jn...]
    unnamed x159 -> x253, local copies, waits for them, and re-layouts: 15 us -> 21.7 us
  transfers between devices with their start and end apart: 40 -> 40, of which waited for: 19 -> 19; matrix products, arithmetic and copies ran while one was open for 9% -> 25% of each run, Pallas kernels for 0% -> 0%
where the time goes in v2:
time: 570 us; the launch traced here: 565 us
  waiting for transfers between devices  295 us (52%)
  matrix products  105 us (18%)
  other arithmetic  60.9 us (11%)
  local copies, waits for them, and re-layouts  58 us (10%)
  starting transfers between devices  29.2 us (5%)
  between operations  15.9 us (3%)
    all_gather x1, waiting for transfers between devices, local(): lax.all_gather(jnp.concatenate([w_query, w_key, w_value, w_output.T, w_ga...  181 us
    ppermute x39, waiting for transfers between devices, swap(): return lax.ppermute(values, 'fsdp', partners(device_count, bit))  114 us
    ppermute x39, starting transfers between devices, swap(): return lax.ppermute(values, 'fsdp', partners(device_count, bit))  29.2 us
    dot_general x6, matrix products, back_project(): jnp.einsum('tj,ij->ti', grads, weight, preferred_element_type=jnp.float32)  29.1 us
    dot_general x4, matrix products, apply_projection(): return jnp.dot(left, weight, preferred_element_type=jnp.float32)  24.9 us
    unnamed x253, local copies, waits for them, and re-layouts  21.7 us
    dot_general x12, matrix products, contract(): jnp.einsum('ti,tj->ij', left, right, preferred_element_type=jnp.float32)  21.4 us
    concatenate x6, other arithmetic, both(): return jnp.concatenate([values, swap(values, device_count, 0)], axis=0)  14.7 us
  transfers between devices with their start and end apart: 40, of which 19 were waited for; matrix products, arithmetic and copies ran while one was open for 25% of the time, Pallas kernels for 0%

profile of v2, /device:TPU:0, one launch (start us, length us, event | category | flops | bytes accessed | tf_op | source)
XLA Modules:
  0.0 564.5 jit_solution(7502760742701743936)
XLA Ops:
  23.1 181.2 %all-gather.2.cloned.1.call-done = bf16[1024,15488]{1,0:T(8,128)(2,1)} async-done(((bf16[32,15488]{1,0:T(8,128)(2,1)}), bf16[1024,15488]{1,0:T(8,128)(2,1)}) %all-gather.2.cloned.1.call-update) | async-done | bytes 31719440 | tf_op jit(solution)/shard_map/all_gather | solution.py:187
  206.6 5.8 %fusion.4 = f32[256,4096]{1,0:T(8,128)S(1)} fusion(bf16[1024,15488]{1,0:T(8,128)(2,1)} %all-gather.2.cloned.1.call-done, bf16[256,1024]{1,0:T(8,128)(2,1)S(1)} %copy-done.46, f32[1024]{0:T(1024)S(1)} %get-tuple-element.93, f32[256]{0:T(256)S(1)} %add_rsqrt_fusion.3), kind=kOutput, calls=%fused_computation.5 | convolution fusion | flops 2148532224 | bytes 13112320 | tf_op jit(solution)/shard_map/dot_general | solution.py:61
  218.8 2.4 copy.174
  231.4 5.5 fusion.172
  236.9 4.0 convolution_convert_fusion.6
  241.1 4.0 multiply_reduce_fusion.7
  246.9 6.7 %fusion.2 = f32[256,6144]{1,0:T(8,128)S(1)} fusion(bf16[256,1024]{1,0:T(8,128)(2,1)S(1)} %multiply_convert_fusion.5, bf16[1024,15488]{1,0:T(8,128)(2,1)} %all-gather.2.cloned.1.call-done), kind=kOutput, calls=%fused_computation.3 | convolution fusion | flops 3221225472 | bytes 19398656 | tf_op jit(solution)/shard_map/dot_general | solution.py:61
  253.6 8.0 %multiply_convert_fusion.2 = (bf16[256,3072]{1,0:T(8,128)(2,1)}, bf16[256,3072]{1,0:T(8,128)(2,1)}, bf16[256,3072]{1,0:T(8,128)(2,1)}) fusion(f32[256,6144]{1,0:T(8,128)S(1)} %fusion.2, bf16[1024,15488]{1,0:T(8,128)(2,1)} %all-gather.2.cloned.1.call-done, bf16[256,1024]{1,0:T(8,128)(2,1)S(1)} %copy-done.42, f32[256]{0:T(256)S(1)} %copy-done.98), kind=kOutput, calls=%fused_computation.42 | convolution fusion | flops 1623195648 | bytes 17826816 | tf_op jit(solution)/shard_map/dot_general | solution.py:61
  262.7 5.9 %fusion.58 = bf16[256,1024]{1,0:T(8,128)(2,1)} fusion(f32[256,1024]{1,0:T(8,128)S(1)} %get-tuple-element.99, bf16[256,3072]{1,0:T(8,128)(2,1)} %get-tuple-element.79, bf16[1024,15488]{1,0:T(8,128)(2,1)} %all-gather.2.cloned.1.call-done, f32[256]{0:T(256)S(1)} %copy-done.98), kind=kOutput, calls=%fused_computation.106 | convolution fusion | flops 1611399168 | bytes 9438208 | tf_op jit(solution)/shard_map/tj,ij->ti/dot_general | solution.py:65
  268.6 5.1 fusion.6
  273.7 6.1 %fusion.55 = f32[256,1024]{1,0:T(8,128)} fusion(f32[256,1024]{1,0:T(8,128)S(1)} %fusion.6, bf16[256,3072]{1,0:T(8,128)(2,1)} %get-tuple-element.77, bf16[1024,15488]{1,0:T(8,128)(2,1)} %all-gather.2.cloned.1.call-done), kind=kOutput, calls=%fused_computation.105 | convolution fusion | flops 1610874880 | bytes 9961472 | tf_op jit(solution)/shard_map/tj,ij->ti/dot_general | solution.py:65
  283.9 3.1 copy.158
  291.2 3.0 pad_maximum_fusion.3
  296.4 3.2 pad_maximum_fusion.1
  299.6 3.2 pad_maximum_fusion
  303.4 2.1 convolution_convert_fusion
  306.1 2.2 convolution_convert_fusion.1
  310.3 2.2 convolution_convert_fusion.2
  316.0 4.4 fusion.27
  320.4 2.5 copy.178
  323.0 2.2 fusion.106
  330.2 12.2 %collective-permute-done.10 = bf16[256,3072]{1,0:T(8,128)(2,1)} collective-permute-done((bf16[256,3072]{1,0:T(8,128)(2,1)}, bf16[256,3072]{1,0:T(8,128)(2,1)}, u32[]{:S(2)}, u32[]{:S(2)}) %collective-permute-start.10) | collective-permute-done | bytes 1572896 | tf_op jit(solution)/shard_map/ppermute | solution.py:131
  342.4 2.7 collective-permute-done.9
  345.2 4.0 collective-permute-done.8
  352.2 2.6 convert_add_fusion
  355.6 3.1 convert_add_fusion.1
  359.9 2.5 convert_add_fusion.2
  369.6 5.9 %collective-permute-done.13 = bf16[128,3072]{1,0:T(8,128)(2,1)S(1)} collective-permute-done((bf16[128,3072]{1,0:T(8,128)(2,1)S(1)}, bf16[128,3072]{1,0:T(8,128)(2,1)S(1)}, u32[]{:S(2)}, u32[]{:S(2)}) %collective-permute-start.13) | collective-permute-done | bytes 786464 | tf_op jit(solution)/shard_map/ppermute | solution.py:131
  375.5 14.3 %collective-permute-done.12 = bf16[128,3072]{1,0:T(8,128)(2,1)S(1)} collective-permute-done((bf16[128,3072]{1,0:T(8,128)(2,1)S(1)}, bf16[128,3072]{1,0:T(8,128)(2,1)S(1)}, u32[]{:S(2)}, u32[]{:S(2)}) %collective-permute-start.12) | collective-permute-done | bytes 786464 | tf_op jit(solution)/shard_map/ppermute | solution.py:131
  392.0 3.5 copy.153
  397.2 2.7 fusion.167
  399.9 3.5 copy.155
  403.4 4.2 pad_maximum_fusion.4
  407.6 3.5 copy.156
  431.1 4.3 fusion.32
  435.3 3.5 fusion.14
  453.2 10.0 %collective-permute-done.33 = bf16[32,3072]{1,0:T(8,128)(2,1)S(1)} collective-permute-done((bf16[32,3072]{1,0:T(8,128)(2,1)S(1)}, bf16[32,3072]{1,0:T(8,128)(2,1)S(1)}, u32[]{:S(2)}, u32[]{:S(2)}) %collective-permute-start.33) | collective-permute-done | bytes 196640 | tf_op jit(solution)/shard_map/ppermute | solution.py:131
  465.0 2.4 collective-permute-done.32
  468.3 5.7 %collective-permute-done.31 = bf16[32,3072]{1,0:T(8,128)(2,1)S(1)} collective-permute-done((bf16[32,3072]{1,0:T(8,128)(2,1)S(1)}, bf16[32,3072]{1,0:T(8,128)(2,1)S(1)}, u32[]{:S(2)}, u32[]{:S(2)}) %collective-permute-start.31) | collective-permute-done | bytes 196640 | tf_op jit(solution)/shard_map/ppermute | solution.py:131
  478.9 4.6 fusion.83
  484.4 3.3 collective-permute-done.25
  492.8 2.3 collective-permute-done.35
  496.0 2.6 collective-permute-done.36
  500.7 24.2 %collective-permute-done.37 = f32[2,72]{1,0:T(2,128)S(1)} collective-permute-done((f32[2,72]{1,0:T(2,128)S(1)}, f32[2,72]{1,0:T(2,128)S(1)}, u32[]{:S(2)}, u32[]{:S(2)}) %collective-permute-start.37) | collective-permute-done | bytes 608 | tf_op jit(solution)/shard_map/ppermute | solution.py:131
  528.6 5.3 collective-permute-done.27
  535.0 5.6 collective-permute-done.22
  542.7 6.1 %collective-permute-done.23 = bf16[64,2048]{1,0:T(8,128)(2,1)S(1)} collective-permute-done((bf16[64,2048]{1,0:T(8,128)(2,1)S(1)}, bf16[64,2048]{1,0:T(8,128)(2,1)S(1)}, u32[]{:S(2)}, u32[]{:S(2)}) %collective-permute-start.23) | collective-permute-done | bytes 262176 | tf_op jit(solution)/shard_map/ppermute | solution.py:131
  551.5 5.2 collective-permute-done.24
  (462 shorter events, 136.2 us)
Async XLA Ops:
  7.2 197.1 %all-gather.2.cloned.1.call-start = ((), (), s32[]{:S(2)}) async-start(), calls=%async_computation | async-start | bytes 32710656 | tf_op jit(solution)/shard_map/all_gather | solution.py:187
  16.3 6.0 %collective-permute-start.1 = (bf16[256,512]{1,0:T(8,128)(2,1)S(1)}, bf16[256,512]{1,0:T(8,128)(2,1)S(1)}, u32[]{:S(2)}, u32[]{:S(2)}) collective-permute-start(bf16[256,512]{1,0:T(8,128)(2,1)S(1)} %fusion.74), channel_id=1, source_target_pairs={{0,1},{1,0},{2,3},{3,2},{4,5},{5,4},{6,7},{7,6},{8,9},{9,8},{10,11... | collective-permute-start | bytes 786440 | tf_op jit(solution)/shard_map/ppermute | solution.py:131
  19.5 187.1 %copy-start.100 = (f32[256]{0:T(256)}, f32[256]{0:T(256)S(1)}, u32[]{:S(2)}) copy-start(f32[256]{0:T(256)S(1)} %add_rsqrt_fusion.3) | copy-start | bytes 3076
  240.8 50.4 %collective-permute-start.6 = (bf16[256,2048]{0,1:T(8,128)(2,1)}, bf16[256,2048]{0,1:T(8,128)(2,1)}, u32[]{:S(2)}, u32[]{:S(2)}) collective-permute-start(bf16[256,2048]{0,1:T(8,128)(2,1)} %bitcast.16), channel_id=1, source_target_pairs={{0,1},{1,0},{2,3},{3,2},{4,5},{5,4},{6,7},{7,6},{8,9},{9,8},{10,11... | collective-permute-start | bytes 3145736 | tf_op jit(solution)/shard_map/ppermute | solution.py:131
  245.0 17.6 %copy-start.10 = (f32[256,1024]{1,0:T(8,128)}, f32[256,1024]{1,0:T(8,128)S(1)}, u32[]{:S(2)}) copy-start(f32[256,1024]{1,0:T(8,128)S(1)} %get-tuple-element.99) | copy-start | bytes 3145732
  261.6 32.6 %collective-permute-start.4 = (bf16[256,3072]{1,0:T(8,128)(2,1)}, bf16[256,3072]{1,0:T(8,128)(2,1)}, u32[]{:S(2)}, u32[]{:S(2)}) collective-permute-start(bf16[256,3072]{1,0:T(8,128)(2,1)} %get-tuple-element.78), channel_id=1, source_target_pairs={{0,1},{1,0},{2,3},{3,2},{4,5},{5,4},{6,7},{7,6},{8,9},{9,8},{10,11... | collective-permute-start | bytes 4718600 | tf_op jit(solution)/shard_map/ppermute | solution.py:131
  261.9 34.5 %collective-permute-start.3 = (bf16[256,3072]{1,0:T(8,128)(2,1)}, bf16[256,3072]{1,0:T(8,128)(2,1)}, u32[]{:S(2)}, u32[]{:S(2)}) collective-permute-start(bf16[256,3072]{1,0:T(8,128)(2,1)} %get-tuple-element.77), channel_id=1, source_target_pairs={{0,1},{1,0},{2,3},{3,2},{4,5},{5,4},{6,7},{7,6},{8,9},{9,8},{10,11... | collective-permute-start | bytes 4718600 | tf_op jit(solution)/shard_map/ppermute | solution.py:131
  262.1 37.5 %collective-permute-start.2 = (bf16[256,3072]{1,0:T(8,128)(2,1)}, bf16[256,3072]{1,0:T(8,128)(2,1)}, u32[]{:S(2)}, u32[]{:S(2)}) collective-permute-start(bf16[256,3072]{1,0:T(8,128)(2,1)} %get-tuple-element.79), channel_id=1, source_target_pairs={{0,1},{1,0},{2,3},{3,2},{4,5},{5,4},{6,7},{7,6},{8,9},{9,8},{10,11... | collective-permute-start | bytes 4718600 | tf_op jit(solution)/shard_map/ppermute | solution.py:131
  262.4 26.4 %collective-permute-start = (bf16[256,512]{1,0:T(8,128)(2,1)}, bf16[256,512]{1,0:T(8,128)(2,1)}, u32[]{:S(2)}, u32[]{:S(2)}) collective-permute-start(bf16[256,512]{1,0:T(8,128)(2,1)} %fusion.73), channel_id=1, source_target_pairs={{0,1},{1,0},{2,3},{3,2},{4,5},{5,4},{6,7},{7,6},{8,9},{9,8},{10,11... | collective-permute-start | bytes 786440 | tf_op jit(solution)/shard_map/ppermute | solution.py:131
  288.8 1.6 collective-permute-start.7
  299.6 10.7 %copy-start = (bf16[512,3072]{1,0:T(8,128)(2,1)}, bf16[512,3072]{1,0:T(8,128)(2,1)S(1)}, u32[]{:S(2)}) copy-start(bf16[512,3072]{1,0:T(8,128)(2,1)S(1)} %pad_maximum_fusion.1) | copy-start | bytes 9437188
  305.6 36.9 %collective-permute-start.10 = (bf16[256,3072]{1,0:T(8,128)(2,1)}, bf16[256,3072]{1,0:T(8,128)(2,1)}, u32[]{:S(2)}, u32[]{:S(2)}) collective-permute-start(bf16[256,3072]{1,0:T(8,128)(2,1)} %convolution_convert_fusion), channel_id=1, source_target_pairs={{0,8},{1,9},{2,10},{3,11},{4,12},{5,13},{6,14},{7,15},{8,0},{9,1},... | collective-permute-start | bytes 4718600 | tf_op jit(solution)/shard_map/ppermute | solution.py:131
  308.3 36.9 %collective-permute-start.9 = (bf16[256,3072]{1,0:T(8,128)(2,1)}, bf16[256,3072]{1,0:T(8,128)(2,1)}, u32[]{:S(2)}, u32[]{:S(2)}) collective-permute-start(bf16[256,3072]{1,0:T(8,128)(2,1)} %convolution_convert_fusion.1), channel_id=1, source_target_pairs={{0,4},{1,5},{2,6},{3,7},{4,0},{5,1},{6,2},{7,3},{8,12},{9,13},{10,... | collective-permute-start | bytes 4718600 | tf_op jit(solution)/shard_map/ppermute | solution.py:131
  312.5 36.6 %collective-permute-start.8 = (bf16[256,3072]{1,0:T(8,128)(2,1)}, bf16[256,3072]{1,0:T(8,128)(2,1)}, u32[]{:S(2)}, u32[]{:S(2)}) collective-permute-start(bf16[256,3072]{1,0:T(8,128)(2,1)} %convolution_convert_fusion.2), channel_id=1, source_target_pairs={{0,2},{1,3},{2,0},{3,1},{4,6},{5,7},{6,4},{7,5},{8,10},{9,11},{10,... | collective-permute-start | bytes 4718600 | tf_op jit(solution)/shard_map/ppermute | solution.py:131
  316.0 13.1 %collective-permute-start.5 = (bf16[256,512]{1,0:T(8,128)(2,1)}, bf16[256,512]{1,0:T(8,128)(2,1)}, u32[]{:S(2)}, u32[]{:S(2)}) collective-permute-start(bf16[256,512]{1,0:T(8,128)(2,1)} %fusion.75), channel_id=1, source_target_pairs={{0,1},{1,0},{2,3},{3,2},{4,5},{5,4},{6,7},{7,6},{8,9},{9,8},{10,11... | collective-permute-start | bytes 786440 | tf_op jit(solution)/shard_map/ppermute | solution.py:131
  328.6 20.6 %copy-start.109 = (s32[512]{0:T(512)S(1)}, s32[512]{0:T(512)}, u32[]{:S(2)}) copy-start(s32[512]{0:T(512)} %multiply_add_fusion) | copy-start | bytes 6148
  328.6 21.1 %copy-start.7 = (bf16[512,2048]{0,1:T(8,128)(2,1)S(1)}, bf16[512,2048]{0,1:T(8,128)(2,1)}, u32[]{:S(2)}) copy-start(bf16[512,2048]{0,1:T(8,128)(2,1)} %pad_maximum_fusion.3) | copy-start | bytes 6291460
  330.2 22.0 %copy-start.5 = (bf16[512,3072]{1,0:T(8,128)(2,1)S(1)}, bf16[512,3072]{1,0:T(8,128)(2,1)}, u32[]{:S(2)}) copy-start(bf16[512,3072]{1,0:T(8,128)(2,1)} %copy-done.4) | copy-start | bytes 9437188
  330.2 22.0 %copy-start.61 = (bf16[512,512]{1,0:T(8,128)(2,1)S(1)}, bf16[512,512]{1,0:T(8,128)(2,1)}, u32[]{:S(2)}) copy-start(bf16[512,512]{1,0:T(8,128)(2,1)} %copy-done.60) | copy-start | bytes 1572868
  350.4 39.5 %collective-permute-start.14 = (bf16[256,2048]{1,0:T(8,128)(2,1)S(1)}, bf16[256,2048]{1,0:T(8,128)(2,1)S(1)}, u32[]{:S(2)}, u32[]{:S(2)}) collective-permute-start(bf16[256,2048]{1,0:T(8,128)(2,1)S(1)} %convolution_convert_fusion.5), channel_id=1, source_target_pairs={{0,8},{1,9},{2,10},{3,11},{4,12},{5,13},{6,14},{7,15},{8,0},{9,1},... | collective-permute-start | bytes 3145736 | tf_op jit(solution)/shard_map/ppermute | solution.py:131
  355.0 20.5 %collective-permute-start.13 = (bf16[128,3072]{1,0:T(8,128)(2,1)S(1)}, bf16[128,3072]{1,0:T(8,128)(2,1)S(1)}, u32[]{:S(2)}, u32[]{:S(2)}) collective-permute-start(bf16[128,3072]{1,0:T(8,128)(2,1)S(1)} %slice.585), channel_id=1, source_target_pairs={{0,2},{1,3},{2,0},{3,1},{4,6},{5,7},{6,4},{7,5},{8,10},{9,11},{10,... | collective-permute-start | bytes 2359304 | tf_op jit(solution)/shard_map/ppermute | solution.py:131
  358.8 31.0 %collective-permute-start.12 = (bf16[128,3072]{1,0:T(8,128)(2,1)S(1)}, bf16[128,3072]{1,0:T(8,128)(2,1)S(1)}, u32[]{:S(2)}, u32[]{:S(2)}) collective-permute-start(bf16[128,3072]{1,0:T(8,128)(2,1)S(1)} %slice.586), channel_id=1, source_target_pairs={{0,2},{1,3},{2,0},{3,1},{4,6},{5,7},{6,4},{7,5},{8,10},{9,11},{10,... | collective-permute-start | bytes 2359304 | tf_op jit(solution)/shard_map/ppermute | solution.py:131
  362.6 27.3 %collective-permute-start.11 = (bf16[128,3072]{1,0:T(8,128)(2,1)S(1)}, bf16[128,3072]{1,0:T(8,128)(2,1)S(1)}, u32[]{:S(2)}, u32[]{:S(2)}) collective-permute-start(bf16[128,3072]{1,0:T(8,128)(2,1)S(1)} %slice.587), channel_id=1, source_target_pairs={{0,4},{1,5},{2,6},{3,7},{4,0},{5,1},{6,2},{7,3},{8,12},{9,13},{10,... | collective-permute-start | bytes 2359304 | tf_op jit(solution)/shard_map/ppermute | solution.py:131
  375.5 14.4 %copy-start.62 = (bf16[128,3072]{1,0:T(8,128)(2,1)}, bf16[128,3072]{1,0:T(8,128)(2,1)S(1)}, u32[]{:S(2)}) copy-start(bf16[128,3072]{1,0:T(8,128)(2,1)S(1)} %collective-permute-done.13) | copy-start | bytes 2359300
  416.3 24.1 %collective-permute-start.19 = (bf16[128,2048]{1,0:T(8,128)(2,1)}, bf16[128,2048]{1,0:T(8,128)(2,1)}, u32[]{:S(2)}, u32[]{:S(2)}) collective-permute-start(bf16[128,2048]{1,0:T(8,128)(2,1)} %slice.590), channel_id=1, source_target_pairs={{0,2},{1,3},{2,0},{3,1},{4,6},{5,7},{6,4},{7,5},{8,10},{9,11},{10,... | collective-permute-start | bytes 1572872 | tf_op jit(solution)/shard_map/ppermute | solution.py:131
  418.6 21.7 %collective-permute-start.18 = (bf16[64,3072]{1,0:T(8,128)(2,1)}, bf16[64,3072]{1,0:T(8,128)(2,1)}, u32[]{:S(2)}, u32[]{:S(2)}) collective-permute-start(bf16[64,3072]{1,0:T(8,128)(2,1)} %slice.591), channel_id=1, source_target_pairs={{0,4},{1,5},{2,6},{3,7},{4,0},{5,1},{6,2},{7,3},{8,12},{9,13},{10,... | collective-permute-start | bytes 1179656 | tf_op jit(solution)/shard_map/ppermute | solution.py:131
  420.2 20.2 %collective-permute-start.17 = (bf16[64,3072]{1,0:T(8,128)(2,1)}, bf16[64,3072]{1,0:T(8,128)(2,1)}, u32[]{:S(2)}, u32[]{:S(2)}) collective-permute-start(bf16[64,3072]{1,0:T(8,128)(2,1)} %slice.592), channel_id=1, source_target_pairs={{0,8},{1,9},{2,10},{3,11},{4,12},{5,13},{6,14},{7,15},{8,0},{9,1},... | collective-permute-start | bytes 1179656 | tf_op jit(solution)/shard_map/ppermute | solution.py:131
  422.5 17.9 %collective-permute-start.16 = (bf16[64,3072]{1,0:T(8,128)(2,1)}, bf16[64,3072]{1,0:T(8,128)(2,1)}, u32[]{:S(2)}, u32[]{:S(2)}) collective-permute-start(bf16[64,3072]{1,0:T(8,128)(2,1)} %slice.593), channel_id=1, source_target_pairs={{0,8},{1,9},{2,10},{3,11},{4,12},{5,13},{6,14},{7,15},{8,0},{9,1},... | collective-permute-start | bytes 1179656 | tf_op jit(solution)/shard_map/ppermute | solution.py:131
  423.7 15.2 %collective-permute-start.15 = (bf16[256,2048]{0,1:T(8,128)(2,1)S(1)}, bf16[256,2048]{0,1:T(8,128)(2,1)}, u32[]{:S(2)}, u32[]{:S(2)}) collective-permute-start(bf16[256,2048]{0,1:T(8,128)(2,1)S(1)} %pad_maximum_fusion.7), channel_id=1, source_target_pairs={{0,1},{1,0},{2,3},{3,2},{4,5},{5,4},{6,7},{7,6},{8,9},{9,8},{10,11... | collective-permute-start | bytes 3145736 | tf_op jit(solution)/shard_map/ppermute | solution.py:131
  440.4 36.9 %collective-permute-start.20 = (bf16[256,2048]{1,0:T(8,128)(2,1)S(1)}, bf16[256,2048]{1,0:T(8,128)(2,1)S(1)}, u32[]{:S(2)}, u32[]{:S(2)}) collective-permute-start(bf16[256,2048]{1,0:T(8,128)(2,1)S(1)} %fusion.32), channel_id=1, source_target_pairs={{0,1},{1,0},{2,3},{3,2},{4,5},{5,4},{6,7},{7,6},{8,9},{9,8},{10,11... | collective-permute-start | bytes 3145736 | tf_op jit(solution)/shard_map/ppermute | solution.py:131
  441.8 21.3 %collective-permute-start.33 = (bf16[32,3072]{1,0:T(8,128)(2,1)S(1)}, bf16[32,3072]{1,0:T(8,128)(2,1)S(1)}, u32[]{:S(2)}, u32[]{:S(2)}) collective-permute-start(bf16[32,3072]{1,0:T(8,128)(2,1)S(1)} %slice.597), channel_id=1, source_target_pairs={{0,16},{1,17},{2,18},{3,19},{4,20},{5,21},{6,22},{7,23},{8,24},{9,... | collective-permute-start | bytes 589832 | tf_op jit(solution)/shard_map/ppermute | solution.py:131
  444.5 22.9 %collective-permute-start.32 = (bf16[32,3072]{1,0:T(8,128)(2,1)S(1)}, bf16[32,3072]{1,0:T(8,128)(2,1)S(1)}, u32[]{:S(2)}, u32[]{:S(2)}) collective-permute-start(bf16[32,3072]{1,0:T(8,128)(2,1)S(1)} %slice.598), channel_id=1, source_target_pairs={{0,16},{1,17},{2,18},{3,19},{4,20},{5,21},{6,22},{7,23},{8,24},{9,... | collective-permute-start | bytes 589832 | tf_op jit(solution)/shard_map/ppermute | solution.py:131
  447.1 26.9 %collective-permute-start.31 = (bf16[32,3072]{1,0:T(8,128)(2,1)S(1)}, bf16[32,3072]{1,0:T(8,128)(2,1)S(1)}, u32[]{:S(2)}, u32[]{:S(2)}) collective-permute-start(bf16[32,3072]{1,0:T(8,128)(2,1)S(1)} %slice.599), channel_id=1, source_target_pairs={{0,16},{1,17},{2,18},{3,19},{4,20},{5,21},{6,22},{7,23},{8,24},{9,... | collective-permute-start | bytes 589832 | tf_op jit(solution)/shard_map/ppermute | solution.py:131
  449.8 18.3 %collective-permute-start.29 = (bf16[64,2048]{1,0:T(8,128)(2,1)S(1)}, bf16[64,2048]{1,0:T(8,128)(2,1)S(1)}, u32[]{:S(2)}, u32[]{:S(2)}) collective-permute-start(bf16[64,2048]{1,0:T(8,128)(2,1)S(1)} %slice.594), channel_id=1, source_target_pairs={{0,4},{1,5},{2,6},{3,7},{4,0},{5,1},{6,2},{7,3},{8,12},{9,13},{10,... | collective-permute-start | bytes 786440 | tf_op jit(solution)/shard_map/ppermute | solution.py:131
  463.2 24.5 %collective-permute-start.25 = (bf16[256,2048]{1,0:T(8,128)(2,1)}, bf16[256,2048]{1,0:T(8,128)(2,1)}, u32[]{:S(2)}, u32[]{:S(2)}) collective-permute-start(bf16[256,2048]{1,0:T(8,128)(2,1)} %convolution_convert_fusion.3), channel_id=1, source_target_pairs={{0,4},{1,5},{2,6},{3,7},{4,0},{5,1},{6,2},{7,3},{8,12},{9,13},{10,... | collective-permute-start | bytes 3145736 | tf_op jit(solution)/shard_map/ppermute | solution.py:131
  468.2 8.3 %collective-permute-start.30 = (bf16[32,2048]{1,0:T(8,128)(2,1)S(1)}, bf16[32,2048]{1,0:T(8,128)(2,1)S(1)}, u32[]{:S(2)}, u32[]{:S(2)}) collective-permute-start(bf16[32,2048]{1,0:T(8,128)(2,1)S(1)} %slice.600), channel_id=1, source_target_pairs={{0,16},{1,17},{2,18},{3,19},{4,20},{5,21},{6,22},{7,23},{8,24},{9,... | collective-permute-start | bytes 393224 | tf_op jit(solution)/shard_map/ppermute | solution.py:131
  484.3 7.0 %collective-permute-start.34 = (f32[16,72]{1,0:T(8,128)S(1)}, f32[16,72]{1,0:T(8,128)S(1)}, u32[]{:S(2)}, u32[]{:S(2)}) collective-permute-start(f32[16,72]{1,0:T(8,128)S(1)} %slice.451), channel_id=1, source_target_pairs={{0,16},{1,17},{2,18},{3,19},{4,20},{5,21},{6,22},{7,23},{8,24},{9,... | collective-permute-start | bytes 13832 | tf_op jit(solution)/shard_map/ppermute | solution.py:131
  489.8 35.2 %collective-permute-start.26 = (bf16[128,2048]{1,0:T(8,128)(2,1)S(1)}, bf16[128,2048]{1,0:T(8,128)(2,1)S(1)}, u32[]{:S(2)}, u32[]{:S(2)}) collective-permute-start(bf16[128,2048]{1,0:T(8,128)(2,1)S(1)} %slice.588), channel_id=1, source_target_pairs={{0,2},{1,3},{2,0},{3,1},{4,6},{5,7},{6,4},{7,5},{8,10},{9,11},{10,... | collective-permute-start | bytes 1572872 | tf_op jit(solution)/shard_map/ppermute | solution.py:131
  491.4 3.7 collective-permute-start.35
  492.2 33.3 %collective-permute-start.21 = (bf16[256,2048]{1,0:T(8,128)(2,1)S(1)}, bf16[256,2048]{1,0:T(8,128)(2,1)S(1)}, u32[]{:S(2)}, u32[]{:S(2)}) collective-permute-start(bf16[256,2048]{1,0:T(8,128)(2,1)S(1)} %convolution_convert_fusion.4), channel_id=1, source_target_pairs={{0,2},{1,3},{2,0},{3,1},{4,6},{5,7},{6,4},{7,5},{8,10},{9,11},{10,... | collective-permute-start | bytes 3145736 | tf_op jit(solution)/shard_map/ppermute | solution.py:131
  495.0 3.6 collective-permute-start.36
  498.6 26.3 %collective-permute-start.37 = (f32[2,72]{1,0:T(2,128)S(1)}, f32[2,72]{1,0:T(2,128)S(1)}, u32[]{:S(2)}, u32[]{:S(2)}) collective-permute-start(f32[2,72]{1,0:T(2,128)S(1)} %slice.368), channel_id=1, source_target_pairs={{0,2},{1,3},{2,0},{3,1},{4,6},{5,7},{6,4},{7,5},{8,10},{9,11},{10,... | collective-permute-start | bytes 1736 | tf_op jit(solution)/shard_map/ppermute | solution.py:131
  524.9 3.1 collective-permute-start.38
  525.1 8.8 %collective-permute-start.27 = (bf16[64,2048]{1,0:T(8,128)(2,1)S(1)}, bf16[64,2048]{1,0:T(8,128)(2,1)S(1)}, u32[]{:S(2)}, u32[]{:S(2)}) collective-permute-start(bf16[64,2048]{1,0:T(8,128)(2,1)S(1)} %slice.595), channel_id=1, source_target_pairs={{0,8},{1,9},{2,10},{3,11},{4,12},{5,13},{6,14},{7,15},{8,0},{9,1},... | collective-permute-start | bytes 786440 | tf_op jit(solution)/shard_map/ppermute | solution.py:131
  526.3 14.3 %collective-permute-start.22 = (bf16[128,2048]{1,0:T(8,128)(2,1)S(1)}, bf16[128,2048]{1,0:T(8,128)(2,1)S(1)}, u32[]{:S(2)}, u32[]{:S(2)}) collective-permute-start(bf16[128,2048]{1,0:T(8,128)(2,1)S(1)} %slice.589), channel_id=1, source_target_pairs={{0,4},{1,5},{2,6},{3,7},{4,0},{5,1},{6,2},{7,3},{8,12},{9,13},{10,... | collective-permute-start | bytes 1572872 | tf_op jit(solution)/shard_map/ppermute | solution.py:131
  534.0 8.7 %collective-permute-start.28 = (bf16[32,2048]{1,0:T(8,128)(2,1)S(1)}, bf16[32,2048]{1,0:T(8,128)(2,1)S(1)}, u32[]{:S(2)}, u32[]{:S(2)}) collective-permute-start(bf16[32,2048]{1,0:T(8,128)(2,1)S(1)} %slice.601), channel_id=1, source_target_pairs={{0,16},{1,17},{2,18},{3,19},{4,20},{5,21},{6,22},{7,23},{8,24},{9,... | collective-permute-start | bytes 393224 | tf_op jit(solution)/shard_map/ppermute | solution.py:131
  540.8 7.9 %collective-permute-start.23 = (bf16[64,2048]{1,0:T(8,128)(2,1)S(1)}, bf16[64,2048]{1,0:T(8,128)(2,1)S(1)}, u32[]{:S(2)}, u32[]{:S(2)}) collective-permute-start(bf16[64,2048]{1,0:T(8,128)(2,1)S(1)} %slice.596), channel_id=1, source_target_pairs={{0,8},{1,9},{2,10},{3,11},{4,12},{5,13},{6,14},{7,15},{8,0},{9,1},... | collective-permute-start | bytes 786440 | tf_op jit(solution)/shard_map/ppermute | solution.py:131
  548.8 7.9 %collective-permute-start.24 = (bf16[32,2048]{1,0:T(8,128)(2,1)S(1)}, bf16[32,2048]{1,0:T(8,128)(2,1)S(1)}, u32[]{:S(2)}, u32[]{:S(2)}) collective-permute-start(bf16[32,2048]{1,0:T(8,128)(2,1)S(1)} %slice.602), channel_id=1, source_target_pairs={{0,16},{1,17},{2,18},{3,19},{4,20},{5,21},{6,22},{7,23},{8,24},{9,... | collective-permute-start | bytes 393224 | tf_op jit(solution)/shard_map/ppermute | solution.py:131
  (113 other events, 382.8 us)
Sparse Core Ops, SparseCore 0:
  15.5 188.7 all-gather.1

commit v3 on v2

--- a/solution.py
+++ b/solution.py
@@ -31,21 +31,41 @@
     inverse = ROPE_BASE ** (-(jnp.arange(half_width, dtype=jnp.float32) * 2.0 / HEAD_WIDTH))
     angles = position.astype(jnp.float32)[:, None] * inverse[None, :]
     angles = jnp.concatenate([angles, angles], axis=-1)
-    return (jnp.cos(angles)[:, None, :], jnp.sin(angles)[:, None, :])
+    return (jnp.cos(angles)[None], jnp.sin(angles)[None])
+
+
+def turning(dtype=jnp.float32):
+    half_width = HEAD_WIDTH // 2
+    source = jnp.arange(HEAD_WIDTH, dtype=jnp.int32)[:, None]
+    target = jnp.arange(HEAD_WIDTH, dtype=jnp.int32)[None, :]
+    plus = (source == target - half_width).astype(dtype)
+    return plus - (source == target + half_width).astype(dtype)
+
+
+def turn(values, matrix):
+    return jnp.einsum(
+        "htd,de->hte",
+        values,
+        matrix,
+        precision=lax.Precision.HIGHEST,
+        preferred_element_type=jnp.float32,
+    )
 
 
 def apply_rotary(values, cosine_lookup, sine_lookup):
-    half_width = values.shape[-1] // 2
-    turned = jnp.concatenate([-values[..., half_width:], values[..., :half_width]], axis=-1)
-    return values * cosine_lookup + turned * sine_lookup
+    return values * cosine_lookup + turn(values, turning()) * sine_lookup
 
 
 def rotate_back(grads, cosine_lookup, sine_lookup):
-    half_width = grads.shape[-1] // 2
-    turned = grads * sine_lookup
-    return grads * cosine_lookup + jnp.concatenate(
-        [turned[..., half_width:], -turned[..., :half_width]], axis=-1
-    )
+    return grads * cosine_lookup + turn(grads * sine_lookup, turning().T)
+
+
+def heads_first(values):
+    return values.reshape(values.shape[0], -1, HEAD_WIDTH).transpose(1, 0, 2)
+
+
+def heads_last(values):
+    return values.transpose(1, 0, 2).reshape(values.shape[1], -1)
 
 
 def normalize(values):
@@ -80,9 +100,9 @@
 
 
 def block_scores(query_block, key_block, seg_rows, seg_keys, first_row):
-    row_count = query_block.shape[0]
-    key_count = key_block.shape[0]
-    raw = jnp.einsum("qkgd,lkd->kgql", query_block, key_block, preferred_element_type=jnp.float32)
+    row_count = query_block.shape[2]
+    key_count = key_block.shape[1]
+    raw = jnp.einsum("kgqd,kld->kgql", query_block, key_block, preferred_element_type=jnp.float32)
     row_at = first_row + jnp.arange(row_count, dtype=jnp.int32)
     key_at = jnp.arange(key_count, dtype=jnp.int32)
     allowed = (seg_rows[:, None] == seg_keys[None, :]) & (row_at[:, None] >= key_at[None, :])
@@ -129,6 +149,27 @@
 
 def swap(values, device_count, bit):
     return lax.ppermute(values, "fsdp", partners(device_count, bit))
+
+
+def gather_by_doubling(shard, device_count, me, order):
+    held = shard
+    done = []
+    for bit in order:
+        arrived = swap(held, device_count, bit)
+        place = sum(1 for other in done if other > bit)
+        upper = ((me >> bit) & 1) == 1
+        held = jnp.stack(
+            [jnp.where(upper, arrived, held), jnp.where(upper, held, arrived)], axis=place
+        )
+        done.append(bit)
+    return held
+
+
+def finish_mates(held, device_count, me):
+    arrived = swap(held, device_count, 0)
+    upper = (me & 1) == 1
+    held = jnp.stack([jnp.where(upper, arrived, held), jnp.where(upper, held, arrived)], axis=-3)
+    return held.reshape(-1, held.shape[-1])
 
 
 class OwnerSum:
@@ -185,25 +226,26 @@
     own_gains = norm_gains.shape[0]
     gain_block = jnp.pad(norm_gains[None, :], ((0, rows - 1), (0, 128 - own_gains)))
     gathered = lax.all_gather(
-        jnp.concatenate(
-            [w_query, w_key, w_value, w_output.T, w_gate, w_up, w_down.T, gain_block], axis=1
-        ),
+        jnp.concatenate([w_query, w_key, w_value, w_gate, w_up, gain_block], axis=1),
         "fsdp",
         axis=0,
         tiled=True,
     )
+    chip_bits = list(range(device_count.bit_length() - 2, 0, -1))
+    out_held = gather_by_doubling(
+        w_output.T, device_count, me, chip_bits[:-2] + [chip_bits[-1], chip_bits[-2]]
+    )
+    down_held = gather_by_doubling(w_down.T, device_count, me, chip_bits)
+    gathered, out_held, down_held = lax.optimization_barrier((gathered, out_held, down_held))
+    out_wt = finish_mates(out_held, device_count, me)
+    down_wt = finish_mates(down_held, device_count, me)
     at = qw + 2 * kw
     qkv_w = gathered[:, :at]
-    out_wt = gathered[:, at : at + qw]
-    at = at + qw
     gate_up_w = gathered[:, at : at + 2 * ff]
     at = at + 2 * ff
-    down_wt = gathered[:, at : at + ff]
-    at = at + ff
     gain_all = gathered[:, at:].reshape(device_count, rows, 128)[:, 0, :own_gains].reshape(-1)
 
     query_group_width = QUERY_HEADS // VALUE_HEADS
-    rows_per_block = token_budget
     attn_gain, ffn_gain, query_norm_weight, key_gain = split_gains(gain_all, model_width)
     segment, position = arrange(seq_lens[0], token_budget)
     live_rows = (segment < SLOTS).astype(jnp.float32)[:, None]
@@ -224,17 +266,15 @@
     unit_in, scale_in = normalize(stream)
     rescaled_input = (unit_in * attn_gain).astype(jnp.bfloat16)
     qkv = apply_projection(rescaled_input, qkv_w)
-    query_unrotated = qkv[:, :qw].reshape(token_budget, QUERY_HEADS, HEAD_WIDTH)
-    key_unrotated = qkv[:, qw : qw + kw].reshape(token_budget, VALUE_HEADS, HEAD_WIDTH)
-    value_reduced = (
-        qkv[:, qw + kw :].astype(jnp.bfloat16).reshape(token_budget, VALUE_HEADS, HEAD_WIDTH)
-    )
+    query_unrotated = heads_first(qkv[:, :qw])
+    key_unrotated = heads_first(qkv[:, qw : qw + kw])
+    value_reduced = heads_first(qkv[:, qw + kw :].astype(jnp.bfloat16))
     query_unit, query_scale = normalize(query_unrotated)
     key_unit, key_scale = normalize(key_unrotated)
     query_rotated = apply_rotary(query_unit * query_norm_weight, cosine_lookup, sine_lookup).astype(
         jnp.bfloat16
     )
-    query_rotated = query_rotated.reshape(token_budget, VALUE_HEADS, query_group_width, HEAD_WIDTH)
+    query_rotated = query_rotated.reshape(VALUE_HEADS, query_group_width, token_budget, HEAD_WIDTH)
     key_rot = apply_rotary(key_unit * key_gain, cosine_lookup, sine_lookup).astype(jnp.bfloat16)
     scores = block_scores(query_rotated, key_rot, segment, segment, 0)
     row_top = jnp.max(scores, axis=-1, keepdims=True)
@@ -243,9 +283,9 @@
     prob_rows = lifted / row_mass
     prob_low = prob_rows.astype(jnp.bfloat16)
     mixed = jnp.einsum(
-        "kgql,lkd->qkgd", prob_low, value_reduced, preferred_element_type=jnp.float32
-    )
-    attended = mixed.reshape(rows_per_block, QUERY_HEADS * HEAD_WIDTH).astype(jnp.bfloat16)
+        "kgql,kld->kgqd", prob_low, value_reduced, preferred_element_type=jnp.float32
+    )
+    attended = heads_last(mixed.reshape(QUERY_HEADS, token_budget, HEAD_WIDTH).astype(jnp.bfloat16))
     branch = back_project(attended, out_wt)
     middle = stream + live_rows * branch
     unit_mid, scale_mid = normalize(middle)
@@ -288,11 +328,11 @@
     left_branch = both_halves(grad_branch)
     both_attended = both(attended)
     left_in = both_halves(rescaled_input)
-    row_gradient = gradient_mixed_values.reshape(
-        rows_per_block, VALUE_HEADS, query_group_width, HEAD_WIDTH
+    row_gradient = heads_first(gradient_mixed_values).reshape(
+        VALUE_HEADS, query_group_width, token_budget, HEAD_WIDTH
     )
     grad_probs = jnp.einsum(
-        "qkgd,lkd->kgql", row_gradient, value_reduced, preferred_element_type=jnp.float32
+        "kgqd,kld->kgql", row_gradient, value_reduced, preferred_element_type=jnp.float32
     )
     centre = jnp.sum(prob_rows * grad_probs, axis=-1, keepdims=True)
     grad_raw = (prob_rows * (grad_probs - centre) * HEAD_WIDTH ** (-0.5)).astype(jnp.bfloat16)
@@ -301,34 +341,28 @@
     )
     sums.append(OwnerSum(exact(left_branch, picks[2]), both_attended, device_count, orders[2]))
     query_grads = jnp.einsum(
-        "kgql,lkd->qkgd", grad_raw, key_rot, preferred_element_type=jnp.float32
+        "kgql,kld->kgqd", grad_raw, key_rot, preferred_element_type=jnp.float32
     )
     grad_keys = jnp.einsum(
-        "kgql,qkgd->lkd", grad_raw, query_rotated, preferred_element_type=jnp.float32
+        "kgql,kgqd->kld", grad_raw, query_rotated, preferred_element_type=jnp.float32
     )
     value_gradient = jnp.einsum(
-        "kgql,qkgd->lkd", prob_low, row_gradient, preferred_element_type=jnp.float32
+        "kgql,kgqd->kld", prob_low, row_gradient, preferred_element_type=jnp.float32
     )
     query_grads, grad_keys, value_gradient = after((query_grads, grad_keys, value_gradient), sums)
     grad_khead = rotate_back(grad_keys, cosine_lookup, sine_lookup)
     grad_key_gain = jnp.sum(grad_khead * key_unit, axis=(0, 1))
-    grad_kraw = (
-        norm_back(grad_khead * key_gain, key_unit, key_scale)
-        .reshape(token_budget, VALUE_HEADS * HEAD_WIDTH)
-        .astype(jnp.bfloat16)
-    )
-    value_raw_gradient = value_gradient.reshape(token_budget, VALUE_HEADS * HEAD_WIDTH).astype(
-        jnp.bfloat16
-    )
+    grad_kraw = heads_last(
+        norm_back(grad_khead * key_gain, key_unit, key_scale).astype(jnp.bfloat16)
+    )
+    value_raw_gradient = heads_last(value_gradient.astype(jnp.bfloat16))
     grad_kv = jnp.concatenate([grad_kraw, value_raw_gradient], axis=1)
     both_kv = both(grad_kv)
-    grad_qrot = query_grads.reshape(token_budget, QUERY_HEADS, HEAD_WIDTH)
+    grad_qrot = query_grads.reshape(QUERY_HEADS, token_budget, HEAD_WIDTH)
     grad_qhead = rotate_back(grad_qrot, cosine_lookup, sine_lookup)
     grad_query_gain = jnp.sum(grad_qhead * query_unit, axis=(0, 1))
-    grad_qraw = (
-        norm_back(grad_qhead * query_norm_weight, query_unit, query_scale)
-        .reshape(token_budget, QUERY_HEADS * HEAD_WIDTH)
-        .astype(jnp.bfloat16)
+    grad_qraw = heads_last(
+        norm_back(grad_qhead * query_norm_weight, query_unit, query_scale).astype(jnp.bfloat16)
     )
     grad_qraw, both_kv = after((grad_qraw, both_kv), sums)
     sums.append(OwnerSum(exact(left_in, picks[1]), both_kv, device_count, orders[1]))

time: 570 us -> 536 us (0.940)
  waiting for transfers between devices: 295 us -> 266 us
  local copies, waits for them, and re-layouts: 58 us -> 32.3 us
  starting transfers between devices: 29.2 us -> 50.6 us
  other arithmetic: 60.9 us -> 45 us
  matrix products: 105 us -> 119 us
    all_gather x1, waiting for transfers between devices: 181 us -> 45.5 us  [local(): lax.all_gather(jnp.concatenate([w_query, w_key, w_value, w_gate, w_up, ga...]
    ppermute x39 -> x49, waiting for transfers between devices: 114 us -> 220 us  [swap(): return lax.ppermute(values, 'fsdp', partners(device_count, bit))]
    ppermute x39 -> x49, starting transfers between devices: 29.2 us -> 50.6 us  [swap(): return lax.ppermute(values, 'fsdp', partners(device_count, bit))]
    dot_general x5 -> x8, matrix products: 11.4 us -> 21.9 us  [the longest x4 11.4 us: turn(): jnp.einsum('htd,de->hte', values, matrix, precision=lax.Precision.HIGHEST...]
    unnamed x253 -> x116, local copies, waits for them, and re-layouts: 21.7 us -> 12.2 us
    reshape x5 -> x1, local copies, waits for them, and re-layouts: 10.9 us -> 2.05 us  [heads_first(): return values.reshape(values.shape[0], -1, HEAD_WIDTH).transpose(1, 0, 2)]
    another operation x1 -> x21, other arithmetic: 0.18 us -> 8.42 us  [the longest x4 3.88 us: finish_mates(): jnp.stack([jnp.where(upper, arrived, held), jnp.where(upper, held, arrive...]
    concatenate x6, other arithmetic: 14.7 us -> 6.63 us  [both(): return jnp.concatenate([values, swap(values, device_count, 0)], axis=0)]
  transfers between devices with their start and end apart: 40 -> 50, of which waited for: 19 -> 27; matrix products, arithmetic and copies ran while one was open for 25% -> 26% of each run, Pallas kernels for 0% -> 0%
where the time goes in v3:
time: 536 us; the launch traced here: 529 us
  waiting for transfers between devices  266 us (50%)
  matrix products  119 us (22%)
  starting transfers between devices  50.6 us (9%)
  other arithmetic  45 us (8%)
  local copies, waits for them, and re-layouts  32.3 us (6%)
  between operations  15.6 us (3%)
    ppermute x49, waiting for transfers between devices, swap(): return lax.ppermute(values, 'fsdp', partners(device_count, bit))  220 us
    ppermute x49, starting transfers between devices, swap(): return lax.ppermute(values, 'fsdp', partners(device_count, bit))  50.6 us
    all_gather x1, waiting for transfers between devices, local(): lax.all_gather(jnp.concatenate([w_query, w_key, w_value, w_gate, w_up, ga...  45.5 us
    dot_general x6, matrix products, back_project(): jnp.einsum('tj,ij->ti', grads, weight, preferred_element_type=jnp.float32)  24.4 us
    dot_general x4, matrix products, apply_projection(): return jnp.dot(left, weight, preferred_element_type=jnp.float32)  24.3 us
    dot_general x12, matrix products, contract(): jnp.einsum('ti,tj->ij', left, right, preferred_element_type=jnp.float32)  22.4 us
    dot_general x14, matrix products, exact(): jnp.dot(left, onehot, preferred_element_type=jnp.float32)  13.4 us
    unnamed x116, local copies, waits for them, and re-layouts  12.2 us
  transfers between devices with their start and end apart: 50, of which 27 were waited for; matrix products, arithmetic and copies ran while one was open for 26% of the time, Pallas kernels for 0%

profile of v3, /device:TPU:0, one launch (start us, length us, event | category | flops | bytes accessed | tf_op | source)
XLA Modules:
  0.0 528.6 jit_solution(7917824414088318150)
XLA Ops:
  13.3 4.1 collective-permute-start
  22.8 6.3 %collective-permute-done = bf16[32,2048]{1,0:T(8,128)(2,1)S(1)} collective-permute-done((bf16[32,2048]{1,0:T(8,128)(2,1)}, bf16[32,2048]{1,0:T(8,128)(2,1)S(1)}, u32[]{:S(2)}, u32[]{:S(2)}) %collective-permute-start) | collective-permute-done | bytes 131104 | tf_op jit(solution)/shard_map/ppermute | solution.py:151
  29.2 3.9 collective-permute-start.1
  33.0 8.1 %collective-permute-done.4 = bf16[32,3072]{1,0:T(8,128)(2,1)S(1)} collective-permute-done((bf16[32,3072]{1,0:T(8,128)(2,1)}, bf16[32,3072]{1,0:T(8,128)(2,1)S(1)}, u32[]{:S(2)}, u32[]{:S(2)}) %collective-permute-start.4) | collective-permute-done | bytes 196640 | tf_op jit(solution)/shard_map/ppermute | solution.py:151
  41.2 2.9 collective-permute-start.5
  44.1 8.3 %collective-permute-done.1 = bf16[2,32,2048]{2,1,0:T(8,128)(2,1)S(1)} collective-permute-done((bf16[2,32,2048]{2,1,0:T(8,128)(2,1)S(1)}, bf16[2,32,2048]{2,1,0:T(8,128)(2,1)S(1)}, u32[]{:S(2)}, u32[]{:S(2)}) %collective-permute-start.1) | collective-permute-done | bytes 262176 | tf_op jit(solution)/shard_map/ppermute | solution.py:151
  54.9 7.7 %collective-permute-done.5 = bf16[2,32,3072]{2,1,0:T(8,128)(2,1)S(1)} collective-permute-done((bf16[2,32,3072]{2,1,0:T(8,128)(2,1)S(1)}, bf16[2,32,3072]{2,1,0:T(8,128)(2,1)S(1)}, u32[]{:S(2)}, u32[]{:S(2)}) %collective-permute-start.5) | collective-permute-done | bytes 393248 | tf_op jit(solution)/shard_map/ppermute | solution.py:151
  65.3 10.7 %collective-permute-done.2 = bf16[2,2,32,2048]{3,2,1,0:T(8,128)(2,1)S(1)} collective-permute-done((bf16[2,2,32,2048]{3,2,1,0:T(8,128)(2,1)}, bf16[2,2,32,2048]{3,2,1,0:T(8,128)(2,1)S(1)}, u32[]{:S(2)}, u32[]{:S(2)}) %collective-permute-start.2) | collective-permute-done | bytes 524320 | tf_op jit(solution)/shard_map/ppermute | solution.py:151
  77.6 8.9 %collective-permute-done.6 = bf16[2,2,32,3072]{3,2,1,0:T(8,128)(2,1)S(1)} collective-permute-done((bf16[2,2,32,3072]{3,2,1,0:T(8,128)(2,1)S(1)}, bf16[2,2,32,3072]{3,2,1,0:T(8,128)(2,1)S(1)}, u32[]{:S(2)}, u32[]{:S(2)}) %collective-permute-start.6) | collective-permute-done | bytes 786464 | tf_op jit(solution)/shard_map/ppermute | solution.py:151
  89.3 21.3 %collective-permute-done.3 = bf16[2,2,2,32,2048]{4,3,2,1,0:T(8,128)(2,1)S(1)} collective-permute-done((bf16[2,2,2,32,2048]{4,3,2,1,0:T(8,128)(2,1)S(1)}, bf16[2,2,2,32,2048]{4,3,2,1,0:T(8,128)(2,1)S(1)}, u32[]{:S(2)}, u32[]{:S(2)}) %collective-permute-start.3) | collective-permute-done | bytes 1048608 | tf_op jit(solution)/shard_map/ppermute | solution.py:151
  112.3 27.6 %collective-permute-done.7 = bf16[2,2,2,32,3072]{4,3,2,1,0:T(8,128)(2,1)S(1)} collective-permute-done((bf16[2,2,2,32,3072]{4,3,2,1,0:T(8,128)(2,1)S(1)}, bf16[2,2,2,32,3072]{4,3,2,1,0:T(8,128)(2,1)S(1)}, u32[]{:S(2)}, u32[]{:S(2)}) %collective-permute-start.7) | collective-permute-done | bytes 1572896 | tf_op jit(solution)/shard_map/ppermute | solution.py:151
  140.4 45.5 %all-gather.2.cloned.1.call-done = bf16[1024,10368]{1,0:T(8,128)(2,1)} async-done(((bf16[32,10368]{1,0:T(8,128)(2,1)}), bf16[1024,10368]{1,0:T(8,128)(2,1)}) %all-gather.2.cloned.1.call-update) | async-done | bytes 21233680 | tf_op jit(solution)/shard_map/all_gather | solution.py:228
  187.0 6.0 %fusion.4 = f32[256,4096]{1,0:T(8,128)S(1)} fusion(bf16[1024,10368]{1,0:T(8,128)(2,1)} %all-gather.2.cloned.1.call-done, bf16[256,1024]{1,0:T(8,128)(2,1)} %param.11, f32[1024]{0:T(1024)S(1)} %get-tuple-element.110, f32[256]{0:T(256)S(1)} %add_rsqrt_fusion.3), kind=kOutput, calls=%fused_computation.5 | convolution fusion | flops 2148532224 | bytes 13112320 | tf_op jit(solution)/shard_map/dot_general | solution.py:81
  196.4 3.5 add_convert_fusion
  199.9 5.4 %fusion.182 = (f32[8,2,256]{2,1,0:T(2,128)}, f32[8,2,256,256]{2,3,1,0:T(8,128)}) fusion(pred[256,256]{0,1:T(8,128)(4,1)S(1)} %fusion.132, bf16[8,2,256,128]{3,2,1,0:T(8,128)(2,1)} %bitcast.310, bf16[8,256,128,1]{2,1,3,0:T(8,128)(2,1)} %fusion.53), kind=kOutput, calls=%fused_computation.343 | convolution fusion | flops 272630016 | bytes 5849088 | tf_op jit(solution)/shard_map/sub | solution.py:281
  209.5 3.8 convolution_convert_fusion.7
  220.5 3.0 pad_maximum_fusion.7
  223.5 2.5 select_bitcast_fusion.3
  226.4 3.5 multiply_reduce_fusion.7
  231.0 10.8 %fusion.2 = f32[256,6144]{1,0:T(8,128)} fusion(bf16[256,1024]{1,0:T(8,128)(2,1)S(1)} %multiply_convert_fusion.7, bf16[1024,10368]{1,0:T(8,128)(2,1)} %all-gather.2.cloned.1.call-done), kind=kOutput, calls=%fused_computation.3 | convolution fusion | flops 3221225472 | bytes 19398656 | tf_op jit(solution)/shard_map/dot_general | solution.py:81
  244.7 6.3 %multiply_convert_fusion.3 = (bf16[256,3072]{1,0:T(8,128)(2,1)S(1)}, bf16[256,3072]{1,0:T(8,128)(2,1)S(1)}, bf16[256,3072]{1,0:T(8,128)(2,1)S(1)}) fusion(f32[256,6144]{1,0:T(8,128)} %fusion.2, bf16[1024,3072]{1,0:T(8,128)(2,1)S(1)} %bitcast.294, bf16[256,1024]{1,0:T(8,128)(2,1)S(1)} %copy-done.21, f32[256]{0:T(256)S(1)} %compare_convert_fusion), kind=kOutput, calls=%fused_computation.35 | convolution fusion | flops 1623195648 | bytes 17826816 | tf_op jit(solution)/shard_map/dot_general | solution.py:81
  251.2 2.6 fusion.51
  254.4 4.6 fusion.6
  259.0 4.6 fusion.45
  265.2 3.3 copy-done.18
  283.7 7.3 %multiply_convert_fusion = bf16[8,2,256,256]{2,3,1,0:T(8,128)(2,1)} fusion(bf16[8,2,256,128]{3,2,1,0:T(8,128)(2,1)} %bitcast.308, bf16[8,256,128,1]{1,2,3,0:T(8,128)(2,1)} %bitcast.313, f32[8,2,256,256]{2,3,1,0:T(8,128)} %get-tuple-element.114, f32[8,2,256]{2,1,0:T(2,128)S(1)} %copy-done.54), kind=kOutput, calls=%fused_computation.17 | convolution fusion | flops 544215296 | bytes 7880704 | tf_op jit(solution)/shard_map/sub | solution.py:338
  291.0 4.1 convolution_bitcast_fusion
  296.7 16.7 %collective-permute-done.20 = bf16[256,3072]{1,0:T(8,128)(2,1)} collective-permute-done((bf16[256,3072]{1,0:T(8,128)(2,1)}, bf16[256,3072]{1,0:T(8,128)(2,1)}, u32[]{:S(2)}, u32[]{:S(2)}) %collective-permute-start.20) | collective-permute-done | bytes 1572896 | tf_op jit(solution)/shard_map/ppermute | solution.py:151
  315.8 2.7 collective-permute-done.18
  318.5 2.5 convert_add_fusion
  321.0 2.6 convert_add_fusion.2
  323.6 2.5 convert_add_fusion.1
  337.9 9.5 %collective-permute-done.23 = bf16[128,3072]{1,0:T(8,128)(2,1)S(1)} collective-permute-done((bf16[128,3072]{1,0:T(8,128)(2,1)S(1)}, bf16[128,3072]{1,0:T(8,128)(2,1)S(1)}, u32[]{:S(2)}, u32[]{:S(2)}) %collective-permute-start.23) | collective-permute-done | bytes 786464 | tf_op jit(solution)/shard_map/ppermute | solution.py:151
  347.4 14.6 %collective-permute-done.22 = bf16[128,3072]{1,0:T(8,128)(2,1)S(1)} collective-permute-done((bf16[128,3072]{1,0:T(8,128)(2,1)S(1)}, bf16[128,3072]{1,0:T(8,128)(2,1)S(1)}, u32[]{:S(2)}, u32[]{:S(2)}) %collective-permute-start.22) | collective-permute-done | bytes 786464 | tf_op jit(solution)/shard_map/ppermute | solution.py:151
  368.3 3.5 multiply_reduce_fusion.3
  371.7 2.5 fusion.90
  391.7 2.4 multiply_reduce_fusion.1
  394.1 4.5 fusion.10
  416.1 11.8 %collective-permute-done.43 = bf16[32,3072]{1,0:T(8,128)(2,1)S(1)} collective-permute-done((bf16[32,3072]{1,0:T(8,128)(2,1)S(1)}, bf16[32,3072]{1,0:T(8,128)(2,1)S(1)}, u32[]{:S(2)}, u32[]{:S(2)}) %collective-permute-start.43) | collective-permute-done | bytes 196640 | tf_op jit(solution)/shard_map/ppermute | solution.py:151
  428.7 3.4 collective-permute-done.42
  433.0 5.7 %collective-permute-done.41 = bf16[32,3072]{1,0:T(8,128)(2,1)S(1)} collective-permute-done((bf16[32,3072]{1,0:T(8,128)(2,1)S(1)}, bf16[32,3072]{1,0:T(8,128)(2,1)S(1)}, u32[]{:S(2)}, u32[]{:S(2)}) %collective-permute-start.41) | collective-permute-done | bytes 196640 | tf_op jit(solution)/shard_map/ppermute | solution.py:151
  443.7 4.6 fusion.68
  463.0 24.4 %collective-permute-done.47 = f32[2,72]{1,0:T(2,128)S(1)} collective-permute-done((f32[2,72]{1,0:T(2,128)S(1)}, f32[2,72]{1,0:T(2,128)S(1)}, u32[]{:S(2)}, u32[]{:S(2)}) %collective-permute-start.47) | collective-permute-done | bytes 608 | tf_op jit(solution)/shard_map/ppermute | solution.py:151
  487.6 2.6 collective-permute-start.37
  493.3 3.8 collective-permute-done.37
  499.0 6.1 %collective-permute-done.32 = bf16[128,2048]{1,0:T(8,128)(2,1)S(1)} collective-permute-done((bf16[128,2048]{1,0:T(8,128)(2,1)S(1)}, bf16[128,2048]{1,0:T(8,128)(2,1)S(1)}, u32[]{:S(2)}, u32[]{:S(2)}) %collective-permute-start.32) | collective-permute-done | bytes 524320 | tf_op jit(solution)/shard_map/ppermute | solution.py:151
  506.4 6.6 %collective-permute-done.33 = bf16[64,2048]{1,0:T(8,128)(2,1)S(1)} collective-permute-done((bf16[64,2048]{1,0:T(8,128)(2,1)S(1)}, bf16[64,2048]{1,0:T(8,128)(2,1)S(1)}, u32[]{:S(2)}, u32[]{:S(2)}) %collective-permute-start.33) | collective-permute-done | bytes 262176 | tf_op jit(solution)/shard_map/ppermute | solution.py:151
  514.3 6.4 %collective-permute-done.34 = bf16[32,2048]{1,0:T(8,128)(2,1)S(1)} collective-permute-done((bf16[32,2048]{1,0:T(8,128)(2,1)S(1)}, bf16[32,2048]{1,0:T(8,128)(2,1)S(1)}, u32[]{:S(2)}, u32[]{:S(2)}) %collective-permute-start.34) | collective-permute-done | bytes 131104 | tf_op jit(solution)/shard_map/ppermute | solution.py:151
  (344 shorter events, 147.0 us)
Async XLA Ops:
  7.2 178.7 %all-gather.2.cloned.1.call-start = ((), (), s32[]{:S(2)}) async-start(), calls=%async_computation | async-start | bytes 21897216 | tf_op jit(solution)/shard_map/all_gather | solution.py:228
  13.3 15.8 %collective-permute-start = (bf16[32,2048]{1,0:T(8,128)(2,1)}, bf16[32,2048]{1,0:T(8,128)(2,1)S(1)}, u32[]{:S(2)}, u32[]{:S(2)}) collective-permute-start(bf16[32,2048]{1,0:T(8,128)(2,1)} %bitcast.317), channel_id=1, source_target_pairs={{0,16},{1,17},{2,18},{3,19},{4,20},{5,21},{6,22},{7,23},{8,24},{9,... | collective-permute-start | bytes 393224 | tf_op jit(solution)/shard_map/ppermute | solution.py:151
  17.4 23.7 %collective-permute-start.4 = (bf16[32,3072]{1,0:T(8,128)(2,1)}, bf16[32,3072]{1,0:T(8,128)(2,1)S(1)}, u32[]{:S(2)}, u32[]{:S(2)}) collective-permute-start(bf16[32,3072]{1,0:T(8,128)(2,1)} %bitcast.316), channel_id=1, source_target_pairs={{0,16},{1,17},{2,18},{3,19},{4,20},{5,21},{6,22},{7,23},{8,24},{9,... | collective-permute-start | bytes 589832 | tf_op jit(solution)/shard_map/ppermute | solution.py:151
  20.8 196.2 %collective-permute-start.11 = (bf16[256,512]{1,0:T(8,128)(2,1)}, bf16[256,512]{1,0:T(8,128)(2,1)}, u32[]{:S(2)}, u32[]{:S(2)}) collective-permute-start(bf16[256,512]{1,0:T(8,128)(2,1)} %fusion.59), channel_id=1, source_target_pairs={{0,1},{1,0},{2,3},{3,2},{4,5},{5,4},{6,7},{7,6},{8,9},{9,8},{10,11... | collective-permute-start | bytes 786440 | tf_op jit(solution)/shard_map/ppermute | solution.py:151
  29.2 23.3 %collective-permute-start.1 = (bf16[2,32,2048]{2,1,0:T(8,128)(2,1)S(1)}, bf16[2,32,2048]{2,1,0:T(8,128)(2,1)S(1)}, u32[]{:S(2)}, u32[]{:S(2)}) collective-permute-start(bf16[2,32,2048]{2,1,0:T(8,128)(2,1)S(1)} %pad_maximum_fusion.20), channel_id=1, source_target_pairs={{0,8},{1,9},{2,10},{3,11},{4,12},{5,13},{6,14},{7,15},{8,0},{9,1},... | collective-permute-start | bytes 786440 | tf_op jit(solution)/shard_map/ppermute | solution.py:151
  41.2 21.4 %collective-permute-start.5 = (bf16[2,32,3072]{2,1,0:T(8,128)(2,1)S(1)}, bf16[2,32,3072]{2,1,0:T(8,128)(2,1)S(1)}, u32[]{:S(2)}, u32[]{:S(2)}) collective-permute-start(bf16[2,32,3072]{2,1,0:T(8,128)(2,1)S(1)} %pad_maximum_fusion.19), channel_id=1, source_target_pairs={{0,8},{1,9},{2,10},{3,11},{4,12},{5,13},{6,14},{7,15},{8,0},{9,1},... | collective-permute-start | bytes 1179656 | tf_op jit(solution)/shard_map/ppermute | solution.py:151
  53.3 22.6 %collective-permute-start.2 = (bf16[2,2,32,2048]{3,2,1,0:T(8,128)(2,1)}, bf16[2,2,32,2048]{3,2,1,0:T(8,128)(2,1)S(1)}, u32[]{:S(2)}, u32[]{:S(2)}) collective-permute-start(bf16[2,2,32,2048]{3,2,1,0:T(8,128)(2,1)} %pad_maximum_fusion.14), channel_id=1, source_target_pairs={{0,2},{1,3},{2,0},{3,1},{4,6},{5,7},{6,4},{7,5},{8,10},{9,11},{10,... | collective-permute-start | bytes 1572872 | tf_op jit(solution)/shard_map/ppermute | solution.py:151
  62.8 23.7 %collective-permute-start.6 = (bf16[2,2,32,3072]{3,2,1,0:T(8,128)(2,1)S(1)}, bf16[2,2,32,3072]{3,2,1,0:T(8,128)(2,1)S(1)}, u32[]{:S(2)}, u32[]{:S(2)}) collective-permute-start(bf16[2,2,32,3072]{3,2,1,0:T(8,128)(2,1)S(1)} %pad_maximum_fusion.13), channel_id=1, source_target_pairs={{0,4},{1,5},{2,6},{3,7},{4,0},{5,1},{6,2},{7,3},{8,12},{9,13},{10,... | collective-permute-start | bytes 2359304 | tf_op jit(solution)/shard_map/ppermute | solution.py:151
  76.1 34.4 %collective-permute-start.3 = (bf16[2,2,2,32,2048]{4,3,2,1,0:T(8,128)(2,1)S(1)}, bf16[2,2,2,32,2048]{4,3,2,1,0:T(8,128)(2,1)S(1)}, u32[]{:S(2)}, u32[]{:S(2)}) collective-permute-start(bf16[2,2,2,32,2048]{4,3,2,1,0:T(8,128)(2,1)S(1)} %pad_maximum_fusion.11), channel_id=1, source_target_pairs={{0,4},{1,5},{2,6},{3,7},{4,0},{5,1},{6,2},{7,3},{8,12},{9,13},{10,... | collective-permute-start | bytes 3145736 | tf_op jit(solution)/shard_map/ppermute | solution.py:151
  86.8 53.1 %collective-permute-start.7 = (bf16[2,2,2,32,3072]{4,3,2,1,0:T(8,128)(2,1)S(1)}, bf16[2,2,2,32,3072]{4,3,2,1,0:T(8,128)(2,1)S(1)}, u32[]{:S(2)}, u32[]{:S(2)}) collective-permute-start(bf16[2,2,2,32,3072]{4,3,2,1,0:T(8,128)(2,1)S(1)} %pad_maximum_fusion.10), channel_id=1, source_target_pairs={{0,2},{1,3},{2,0},{3,1},{4,6},{5,7},{6,4},{7,5},{8,10},{9,11},{10,... | collective-permute-start | bytes 4718600 | tf_op jit(solution)/shard_map/ppermute | solution.py:151
  194.0 29.5 %collective-permute-start.9 = (bf16[2,2,2,2,32,2048]{5,4,3,2,1,0:T(8,128)(2,1)}, bf16[2,2,2,2,32,2048]{5,4,3,2,1,0:T(8,128)(2,1)}, u32[]{:S(2)}, u32[]{:S(2)}) collective-permute-start(bf16[2,2,2,2,32,2048]{5,4,3,2,1,0:T(8,128)(2,1)} %pad_maximum_fusion.6), channel_id=1, source_target_pairs={{0,1},{1,0},{2,3},{3,2},{4,5},{5,4},{6,7},{7,6},{8,9},{9,8},{10,11... | collective-permute-start | bytes 6291464 | tf_op jit(solution)/shard_map/ppermute | solution.py:151
  213.3 7.2 %collective-permute-start.16 = (bf16[256,2048]{0,1:T(8,128)(2,1)}, bf16[256,2048]{0,1:T(8,128)(2,1)}, u32[]{:S(2)}, u32[]{:S(2)}) collective-permute-start(bf16[256,2048]{0,1:T(8,128)(2,1)} %bitcast.46), channel_id=1, source_target_pairs={{0,1},{1,0},{2,3},{3,2},{4,5},{5,4},{6,7},{7,6},{8,9},{9,8},{10,11... | collective-permute-start | bytes 3145736 | tf_op jit(solution)/shard_map/ppermute | solution.py:151
  218.8 24.4 %collective-permute-start.8 = (bf16[2,2,2,2,32,3072]{5,4,3,2,1,0:T(8,128)(2,1)S(1)}, bf16[2,2,2,2,32,3072]{5,4,3,2,1,0:T(8,128)(2,1)S(1)}, u32[]{:S(2)}, u32[]{:S(2)}) collective-permute-start(bf16[2,2,2,2,32,3072]{5,4,3,2,1,0:T(8,128)(2,1)S(1)} %pad_maximum_fusion.2), channel_id=1, source_target_pairs={{0,1},{1,0},{2,3},{3,2},{4,5},{5,4},{6,7},{7,6},{8,9},{9,8},{10,11... | collective-permute-start | bytes 9437192 | tf_op jit(solution)/shard_map/ppermute | solution.py:151
  230.7 11.7 %collective-permute-start.10 = (bf16[256,512]{1,0:T(8,128)(2,1)S(1)}, bf16[256,512]{1,0:T(8,128)(2,1)S(1)}, u32[]{:S(2)}, u32[]{:S(2)}) collective-permute-start(bf16[256,512]{1,0:T(8,128)(2,1)S(1)} %fusion.58), channel_id=1, source_target_pairs={{0,1},{1,0},{2,3},{3,2},{4,5},{5,4},{6,7},{7,6},{8,9},{9,8},{10,11... | collective-permute-start | bytes 786440 | tf_op jit(solution)/shard_map/ppermute | solution.py:151
  250.9 12.7 %collective-permute-start.13 = (bf16[256,3072]{1,0:T(8,128)(2,1)S(1)}, bf16[256,3072]{1,0:T(8,128)(2,1)S(1)}, u32[]{:S(2)}, u32[]{:S(2)}) collective-permute-start(bf16[256,3072]{1,0:T(8,128)(2,1)S(1)} %get-tuple-element.82), channel_id=1, source_target_pairs={{0,1},{1,0},{2,3},{3,2},{4,5},{5,4},{6,7},{7,6},{8,9},{9,8},{10,11... | collective-permute-start | bytes 4718600 | tf_op jit(solution)/shard_map/ppermute | solution.py:151
  253.9 10.2 %collective-permute-start.12 = (bf16[256,3072]{1,0:T(8,128)(2,1)S(1)}, bf16[256,3072]{1,0:T(8,128)(2,1)S(1)}, u32[]{:S(2)}, u32[]{:S(2)}) collective-permute-start(bf16[256,3072]{1,0:T(8,128)(2,1)S(1)} %get-tuple-element.84), channel_id=1, source_target_pairs={{0,1},{1,0},{2,3},{3,2},{4,5},{5,4},{6,7},{7,6},{8,9},{9,8},{10,11... | collective-permute-start | bytes 4718600 | tf_op jit(solution)/shard_map/ppermute | solution.py:151
  254.1 9.7 %collective-permute-start.14 = (bf16[256,3072]{1,0:T(8,128)(2,1)S(1)}, bf16[256,3072]{1,0:T(8,128)(2,1)S(1)}, u32[]{:S(2)}, u32[]{:S(2)}) collective-permute-start(bf16[256,3072]{1,0:T(8,128)(2,1)S(1)} %get-tuple-element.83), channel_id=1, source_target_pairs={{0,1},{1,0},{2,3},{3,2},{4,5},{5,4},{6,7},{7,6},{8,9},{9,8},{10,11... | collective-permute-start | bytes 4718600 | tf_op jit(solution)/shard_map/ppermute | solution.py:151
  272.5 23.2 %collective-permute-start.15 = (bf16[256,512]{1,0:T(8,128)(2,1)}, bf16[256,512]{1,0:T(8,128)(2,1)}, u32[]{:S(2)}, u32[]{:S(2)}) collective-permute-start(bf16[256,512]{1,0:T(8,128)(2,1)} %fusion.60), channel_id=1, source_target_pairs={{0,1},{1,0},{2,3},{3,2},{4,5},{5,4},{6,7},{7,6},{8,9},{9,8},{10,11... | collective-permute-start | bytes 786440 | tf_op jit(solution)/shard_map/ppermute | solution.py:151
  276.5 36.9 %collective-permute-start.20 = (bf16[256,3072]{1,0:T(8,128)(2,1)}, bf16[256,3072]{1,0:T(8,128)(2,1)}, u32[]{:S(2)}, u32[]{:S(2)}) collective-permute-start(bf16[256,3072]{1,0:T(8,128)(2,1)} %convolution_convert_fusion), channel_id=1, source_target_pairs={{0,8},{1,9},{2,10},{3,11},{4,12},{5,13},{6,14},{7,15},{8,0},{9,1},... | collective-permute-start | bytes 4718600 | tf_op jit(solution)/shard_map/ppermute | solution.py:151
  278.7 37.0 %collective-permute-start.19 = (bf16[256,3072]{1,0:T(8,128)(2,1)}, bf16[256,3072]{1,0:T(8,128)(2,1)}, u32[]{:S(2)}, u32[]{:S(2)}) collective-permute-start(bf16[256,3072]{1,0:T(8,128)(2,1)} %convolution_convert_fusion.1), channel_id=1, source_target_pairs={{0,4},{1,5},{2,6},{3,7},{4,0},{5,1},{6,2},{7,3},{8,12},{9,13},{10,... | collective-permute-start | bytes 4718600 | tf_op jit(solution)/shard_map/ppermute | solution.py:151
  282.2 36.3 %collective-permute-start.18 = (bf16[256,3072]{1,0:T(8,128)(2,1)}, bf16[256,3072]{1,0:T(8,128)(2,1)}, u32[]{:S(2)}, u32[]{:S(2)}) collective-permute-start(bf16[256,3072]{1,0:T(8,128)(2,1)} %convolution_convert_fusion.2), channel_id=1, source_target_pairs={{0,2},{1,3},{2,0},{3,1},{4,6},{5,7},{6,4},{7,5},{8,10},{9,11},{10,... | collective-permute-start | bytes 4718600 | tf_op jit(solution)/shard_map/ppermute | solution.py:151
  326.9 20.5 %collective-permute-start.23 = (bf16[128,3072]{1,0:T(8,128)(2,1)S(1)}, bf16[128,3072]{1,0:T(8,128)(2,1)S(1)}, u32[]{:S(2)}, u32[]{:S(2)}) collective-permute-start(bf16[128,3072]{1,0:T(8,128)(2,1)S(1)} %slice.504), channel_id=1, source_target_pairs={{0,2},{1,3},{2,0},{3,1},{4,6},{5,7},{6,4},{7,5},{8,10},{9,11},{10,... | collective-permute-start | bytes 2359304 | tf_op jit(solution)/shard_map/ppermute | solution.py:151
  328.5 19.0 %collective-permute-start.21 = (bf16[128,3072]{1,0:T(8,128)(2,1)S(1)}, bf16[128,3072]{1,0:T(8,128)(2,1)S(1)}, u32[]{:S(2)}, u32[]{:S(2)}) collective-permute-start(bf16[128,3072]{1,0:T(8,128)(2,1)S(1)} %slice.506), channel_id=1, source_target_pairs={{0,4},{1,5},{2,6},{3,7},{4,0},{5,1},{6,2},{7,3},{8,12},{9,13},{10,... | collective-permute-start | bytes 2359304 | tf_op jit(solution)/shard_map/ppermute | solution.py:151
  329.8 32.2 %collective-permute-start.22 = (bf16[128,3072]{1,0:T(8,128)(2,1)S(1)}, bf16[128,3072]{1,0:T(8,128)(2,1)S(1)}, u32[]{:S(2)}, u32[]{:S(2)}) collective-permute-start(bf16[128,3072]{1,0:T(8,128)(2,1)S(1)} %slice.505), channel_id=1, source_target_pairs={{0,2},{1,3},{2,0},{3,1},{4,6},{5,7},{6,4},{7,5},{8,10},{9,11},{10,... | collective-permute-start | bytes 2359304 | tf_op jit(solution)/shard_map/ppermute | solution.py:151
  331.0 31.1 %collective-permute-start.24 = (bf16[256,2048]{1,0:T(8,128)(2,1)S(1)}, bf16[256,2048]{1,0:T(8,128)(2,1)S(1)}, u32[]{:S(2)}, u32[]{:S(2)}) collective-permute-start(bf16[256,2048]{1,0:T(8,128)(2,1)S(1)} %convolution_convert_fusion.5), channel_id=1, source_target_pairs={{0,8},{1,9},{2,10},{3,11},{4,12},{5,13},{6,14},{7,15},{8,0},{9,1},... | collective-permute-start | bytes 3145736 | tf_op jit(solution)/shard_map/ppermute | solution.py:151
  381.2 21.7 %collective-permute-start.28 = (bf16[64,3072]{1,0:T(8,128)(2,1)}, bf16[64,3072]{1,0:T(8,128)(2,1)}, u32[]{:S(2)}, u32[]{:S(2)}) collective-permute-start(bf16[64,3072]{1,0:T(8,128)(2,1)} %slice.511), channel_id=1, source_target_pairs={{0,4},{1,5},{2,6},{3,7},{4,0},{5,1},{6,2},{7,3},{8,12},{9,13},{10,... | collective-permute-start | bytes 1179656 | tf_op jit(solution)/shard_map/ppermute | solution.py:151
  382.7 20.2 %collective-permute-start.27 = (bf16[64,3072]{1,0:T(8,128)(2,1)}, bf16[64,3072]{1,0:T(8,128)(2,1)}, u32[]{:S(2)}, u32[]{:S(2)}) collective-permute-start(bf16[64,3072]{1,0:T(8,128)(2,1)} %slice.512), channel_id=1, source_target_pairs={{0,8},{1,9},{2,10},{3,11},{4,12},{5,13},{6,14},{7,15},{8,0},{9,1},... | collective-permute-start | bytes 1179656 | tf_op jit(solution)/shard_map/ppermute | solution.py:151
  384.2 18.7 %collective-permute-start.26 = (bf16[64,3072]{1,0:T(8,128)(2,1)}, bf16[64,3072]{1,0:T(8,128)(2,1)}, u32[]{:S(2)}, u32[]{:S(2)}) collective-permute-start(bf16[64,3072]{1,0:T(8,128)(2,1)} %slice.513), channel_id=1, source_target_pairs={{0,8},{1,9},{2,10},{3,11},{4,12},{5,13},{6,14},{7,15},{8,0},{9,1},... | collective-permute-start | bytes 1179656 | tf_op jit(solution)/shard_map/ppermute | solution.py:151
  386.8 16.1 %collective-permute-start.29 = (bf16[128,2048]{1,0:T(8,128)(2,1)}, bf16[128,2048]{1,0:T(8,128)(2,1)}, u32[]{:S(2)}, u32[]{:S(2)}) collective-permute-start(bf16[128,2048]{1,0:T(8,128)(2,1)} %slice.509), channel_id=1, source_target_pairs={{0,2},{1,3},{2,0},{3,1},{4,6},{5,7},{6,4},{7,5},{8,10},{9,11},{10,... | collective-permute-start | bytes 1572872 | tf_op jit(solution)/shard_map/ppermute | solution.py:151
  389.5 11.9 %collective-permute-start.25 = (bf16[256,2048]{0,1:T(8,128)(2,1)}, bf16[256,2048]{0,1:T(8,128)(2,1)}, u32[]{:S(2)}, u32[]{:S(2)}) collective-permute-start(bf16[256,2048]{0,1:T(8,128)(2,1)} %pad_maximum_fusion.12), channel_id=1, source_target_pairs={{0,1},{1,0},{2,3},{3,2},{4,5},{5,4},{6,7},{7,6},{8,9},{9,8},{10,11... | collective-permute-start | bytes 3145736 | tf_op jit(solution)/shard_map/ppermute | solution.py:151
  407.9 20.0 %collective-permute-start.43 = (bf16[32,3072]{1,0:T(8,128)(2,1)S(1)}, bf16[32,3072]{1,0:T(8,128)(2,1)S(1)}, u32[]{:S(2)}, u32[]{:S(2)}) collective-permute-start(bf16[32,3072]{1,0:T(8,128)(2,1)S(1)} %slice.517), channel_id=1, source_target_pairs={{0,16},{1,17},{2,18},{3,19},{4,20},{5,21},{6,22},{7,23},{8,24},{9,... | collective-permute-start | bytes 589832 | tf_op jit(solution)/shard_map/ppermute | solution.py:151
  409.2 22.9 %collective-permute-start.42 = (bf16[32,3072]{1,0:T(8,128)(2,1)S(1)}, bf16[32,3072]{1,0:T(8,128)(2,1)S(1)}, u32[]{:S(2)}, u32[]{:S(2)}) collective-permute-start(bf16[32,3072]{1,0:T(8,128)(2,1)S(1)} %slice.518), channel_id=1, source_target_pairs={{0,16},{1,17},{2,18},{3,19},{4,20},{5,21},{6,22},{7,23},{8,24},{9,... | collective-permute-start | bytes 589832 | tf_op jit(solution)/shard_map/ppermute | solution.py:151
  410.9 27.8 %collective-permute-start.41 = (bf16[32,3072]{1,0:T(8,128)(2,1)S(1)}, bf16[32,3072]{1,0:T(8,128)(2,1)S(1)}, u32[]{:S(2)}, u32[]{:S(2)}) collective-permute-start(bf16[32,3072]{1,0:T(8,128)(2,1)S(1)} %slice.519), channel_id=1, source_target_pairs={{0,16},{1,17},{2,18},{3,19},{4,20},{5,21},{6,22},{7,23},{8,24},{9,... | collective-permute-start | bytes 589832 | tf_op jit(solution)/shard_map/ppermute | solution.py:151
  412.1 20.7 %collective-permute-start.39 = (bf16[64,2048]{1,0:T(8,128)(2,1)S(1)}, bf16[64,2048]{1,0:T(8,128)(2,1)S(1)}, u32[]{:S(2)}, u32[]{:S(2)}) collective-permute-start(bf16[64,2048]{1,0:T(8,128)(2,1)S(1)} %slice.514), channel_id=1, source_target_pairs={{0,4},{1,5},{2,6},{3,7},{4,0},{5,1},{6,2},{7,3},{8,12},{9,13},{10,... | collective-permute-start | bytes 786440 | tf_op jit(solution)/shard_map/ppermute | solution.py:151
  415.6 33.6 %collective-permute-start.35 = (bf16[256,2048]{1,0:T(8,128)(2,1)}, bf16[256,2048]{1,0:T(8,128)(2,1)}, u32[]{:S(2)}, u32[]{:S(2)}) collective-permute-start(bf16[256,2048]{1,0:T(8,128)(2,1)} %convolution_convert_fusion.3), channel_id=1, source_target_pairs={{0,4},{1,5},{2,6},{3,7},{4,0},{5,1},{6,2},{7,3},{8,12},{9,13},{10,... | collective-permute-start | bytes 3145736 | tf_op jit(solution)/shard_map/ppermute | solution.py:151
  427.9 13.8 %collective-permute-start.30 = (bf16[256,2048]{0,1:T(8,128)(2,1)S(1)}, bf16[256,2048]{0,1:T(8,128)(2,1)S(1)}, u32[]{:S(2)}, u32[]{:S(2)}) collective-permute-start(bf16[256,2048]{0,1:T(8,128)(2,1)S(1)} %bitcast.305), channel_id=1, source_target_pairs={{0,1},{1,0},{2,3},{3,2},{4,5},{5,4},{6,7},{7,6},{8,9},{9,8},{10,11... | collective-permute-start | bytes 3145736 | tf_op jit(solution)/shard_map/ppermute | solution.py:151
  433.0 8.0 %collective-permute-start.40 = (bf16[32,2048]{1,0:T(8,128)(2,1)S(1)}, bf16[32,2048]{1,0:T(8,128)(2,1)S(1)}, u32[]{:S(2)}, u32[]{:S(2)}) collective-permute-start(bf16[32,2048]{1,0:T(8,128)(2,1)S(1)} %slice.520), channel_id=1, source_target_pairs={{0,16},{1,17},{2,18},{3,19},{4,20},{5,21},{6,22},{7,23},{8,24},{9,... | collective-permute-start | bytes 393224 | tf_op jit(solution)/shard_map/ppermute | solution.py:151
  449.2 4.6 collective-permute-start.44
  451.5 35.9 %collective-permute-start.36 = (bf16[128,2048]{1,0:T(8,128)(2,1)S(1)}, bf16[128,2048]{1,0:T(8,128)(2,1)S(1)}, u32[]{:S(2)}, u32[]{:S(2)}) collective-permute-start(bf16[128,2048]{1,0:T(8,128)(2,1)S(1)} %slice.507), channel_id=1, source_target_pairs={{0,2},{1,3},{2,0},{3,1},{4,6},{5,7},{6,4},{7,5},{8,10},{9,11},{10,... | collective-permute-start | bytes 1572872 | tf_op jit(solution)/shard_map/ppermute | solution.py:151
  453.8 3.6 collective-permute-start.45
  457.9 32.3 %collective-permute-start.31 = (bf16[256,2048]{1,0:T(8,128)(2,1)S(1)}, bf16[256,2048]{1,0:T(8,128)(2,1)S(1)}, u32[]{:S(2)}, u32[]{:S(2)}) collective-permute-start(bf16[256,2048]{1,0:T(8,128)(2,1)S(1)} %convolution_convert_fusion.4), channel_id=1, source_target_pairs={{0,2},{1,3},{2,0},{3,1},{4,6},{5,7},{6,4},{7,5},{8,10},{9,11},{10,... | collective-permute-start | bytes 3145736 | tf_op jit(solution)/shard_map/ppermute | solution.py:151
  461.0 26.4 %collective-permute-start.47 = (f32[2,72]{1,0:T(2,128)S(1)}, f32[2,72]{1,0:T(2,128)S(1)}, u32[]{:S(2)}, u32[]{:S(2)}) collective-permute-start(f32[2,72]{1,0:T(2,128)S(1)} %slice.328), channel_id=1, source_target_pairs={{0,2},{1,3},{2,0},{3,1},{4,6},{5,7},{6,4},{7,5},{8,10},{9,11},{10,... | collective-permute-start | bytes 1736 | tf_op jit(solution)/shard_map/ppermute | solution.py:151
  487.4 5.4 %collective-permute-start.48 = (f32[1,72]{1,0:T(1,128)S(1)}, f32[1,72]{1,0:T(1,128)S(1)}, u32[]{:S(2)}, u32[]{:S(2)}) collective-permute-start(f32[1,72]{1,0:T(1,128)S(1)} %slice.330), channel_id=1, source_target_pairs={{0,1},{1,0},{2,3},{3,2},{4,5},{5,4},{6,7},{7,6},{8,9},{9,8},{10,11... | collective-permute-start | bytes 872 | tf_op jit(solution)/shard_map/ppermute | solution.py:151
  487.6 9.5 %collective-permute-start.37 = (bf16[64,2048]{1,0:T(8,128)(2,1)S(1)}, bf16[64,2048]{1,0:T(8,128)(2,1)S(1)}, u32[]{:S(2)}, u32[]{:S(2)}) collective-permute-start(bf16[64,2048]{1,0:T(8,128)(2,1)S(1)} %slice.515), channel_id=1, source_target_pairs={{0,8},{1,9},{2,10},{3,11},{4,12},{5,13},{6,14},{7,15},{8,0},{9,1},... | collective-permute-start | bytes 786440 | tf_op jit(solution)/shard_map/ppermute | solution.py:151
  491.0 14.1 %collective-permute-start.32 = (bf16[128,2048]{1,0:T(8,128)(2,1)S(1)}, bf16[128,2048]{1,0:T(8,128)(2,1)S(1)}, u32[]{:S(2)}, u32[]{:S(2)}) collective-permute-start(bf16[128,2048]{1,0:T(8,128)(2,1)S(1)} %slice.508), channel_id=1, source_target_pairs={{0,4},{1,5},{2,6},{3,7},{4,0},{5,1},{6,2},{7,3},{8,12},{9,13},{10,... | collective-permute-start | bytes 1572872 | tf_op jit(solution)/shard_map/ppermute | solution.py:151
  497.2 9.1 %collective-permute-start.38 = (bf16[32,2048]{1,0:T(8,128)(2,1)S(1)}, bf16[32,2048]{1,0:T(8,128)(2,1)S(1)}, u32[]{:S(2)}, u32[]{:S(2)}) collective-permute-start(bf16[32,2048]{1,0:T(8,128)(2,1)S(1)} %slice.521), channel_id=1, source_target_pairs={{0,16},{1,17},{2,18},{3,19},{4,20},{5,21},{6,22},{7,23},{8,24},{9,... | collective-permute-start | bytes 393224 | tf_op jit(solution)/shard_map/ppermute | solution.py:151
  505.3 7.7 %collective-permute-start.33 = (bf16[64,2048]{1,0:T(8,128)(2,1)S(1)}, bf16[64,2048]{1,0:T(8,128)(2,1)S(1)}, u32[]{:S(2)}, u32[]{:S(2)}) collective-permute-start(bf16[64,2048]{1,0:T(8,128)(2,1)S(1)} %slice.516), channel_id=1, source_target_pairs={{0,8},{1,9},{2,10},{3,11},{4,12},{5,13},{6,14},{7,15},{8,0},{9,1},... | collective-permute-start | bytes 786440 | tf_op jit(solution)/shard_map/ppermute | solution.py:151
  513.1 7.7 %collective-permute-start.34 = (bf16[32,2048]{1,0:T(8,128)(2,1)S(1)}, bf16[32,2048]{1,0:T(8,128)(2,1)S(1)}, u32[]{:S(2)}, u32[]{:S(2)}) collective-permute-start(bf16[32,2048]{1,0:T(8,128)(2,1)S(1)} %slice.522), channel_id=1, source_target_pairs={{0,16},{1,17},{2,18},{3,19},{4,20},{5,21},{6,22},{7,23},{8,24},{9,... | collective-permute-start | bytes 393224 | tf_op jit(solution)/shard_map/ppermute | solution.py:151
  (57 other events, 396.5 us)
Sparse Core Ops, SparseCore 0:
  13.4 172.3 all-gather.1
